TPU v7x, 256 devices: a whole 4x4x8 slice. The times are simulated.
256 devices in a mesh: ctx: 16 (over z_hi, y), head: 16 (over z_lo, x, core).
Axes of the slice: x: 4, y: 4, z: 8 (z_hi: 4, z_lo: 2; z = z_hi * 2 + z_lo), core: 2. Of those that a mesh axis runs over, the one named last changes fastest.
Arguments:
- inputs: bfloat16 [4096, 5376], P('ctx', 'head'), may hold values from -48 to 48
- positions: int32 [4096], P('ctx'), may hold values from 0 to 4095, as said below
- w_query: bfloat16 [5376, 4096], P(None, 'head'), may hold values from -0.125 to 0.125
- w_key: bfloat16 [5376, 2048], P(None, 'head'), may hold values from -0.125 to 0.125
- w_value: bfloat16 [5376, 2048], P(None, 'head'), may hold values from -0.078125 to 0.078125
- w_out: bfloat16 [4096, 5376], P('head'), may hold values from -1 to 1
- post_gain: bfloat16 [5376], P('head'), may hold values from 0.25 to 1.75
- cotangent: bfloat16 [4096, 5376], P('ctx', 'head'), may hold values from -6 to 6
Outputs:
- hidden: bfloat16 [4096, 5376], P('ctx', 'head')
- grad_inputs: bfloat16 [4096, 5376], P('ctx', 'head')
- grad_w_query: float32 [5376, 4096], P('ctx', 'head')
- grad_w_key: float32 [5376, 2048], P('ctx', 'head')
- grad_w_value: float32 [5376, 2048], P('ctx', 'head')
- grad_w_out: float32 [4096, 5376], P('head', 'ctx')
Inputs may be any that keep to these rules, and one draw needn't show every extreme that they name: positions rise by one from each token to the next, except at the first token of a new document, where they are 0; the first token may lie in a document that began earlier.
All inputs are finite; a program needn't handle non-finite values.
Results may differ from a plain program's by a relative error of at most 0.02.
Values may be sent and summed in bfloat16 or wider, within the bound.
A program may use at most 128 MiB of HBM per device.

v0:
```python
import math

import jax
import jax.numpy as jnp
from jax import lax
from jax.sharding import PartitionSpec as P

D = 5376
HEADS = 32
HEAD_DIM = 128
WINDOW = 1024


EPSILON = 1e-06
ROPE_BASE = 10000.0


def shifted(value, axis, steps):
    count = lax.axis_size(axis)
    first, last = (max(0, -steps), min(count, count - steps))
    return lax.ppermute(value, axis, [(source, source + steps) for source in range(first, last)])


def rope_tables(positions, head_dim):
    half_dim = head_dim // 2
    frequency = jnp.exp(
        jnp.arange(half_dim, dtype=jnp.float32) * (-2.0 * math.log(ROPE_BASE) / head_dim)
    )
    angles = positions.astype(jnp.float32)[:, None] * frequency[None, :]
    return (jnp.cos(angles)[:, None, :], jnp.sin(angles)[:, None, :])


def rotate(values, cosine, sine_table):
    half_dim = values.shape[-1] // 2
    first_half = values[..., :half_dim]
    second_half = values[..., half_dim:]
    return jnp.concatenate(
        [
            first_half * cosine - second_half * sine_table,
            second_half * cosine + first_half * sine_table,
        ],
        axis=-1,
    )


def window_mask(query_first, key_first, query_count, key_count, positions, window):
    query_index = query_first + jnp.arange(query_count, dtype=jnp.int32)
    key_index = key_first + jnp.arange(key_count, dtype=jnp.int32)
    distance = query_index[:, None] - key_index[None, :]
    return (
        (key_index[None, :] >= 0)
        & (distance >= 0)
        & (distance < window)
        & (distance <= positions[:, None])
    )


def attend_forward(queries, key_block, value_block, allowed, score_scale):
    scores = (
        jnp.einsum("tkgh,skh->kgts", queries, key_block, preferred_element_type=jnp.float32)
        * score_scale
    )
    scores = jnp.where(allowed, scores, -jnp.inf)
    highest = jnp.max(scores, axis=-1, keepdims=True)
    exponent = jnp.exp(scores - highest)
    probability = exponent / jnp.sum(exponent, axis=-1, keepdims=True)
    weights = probability.astype(jnp.bfloat16)
    attended = jnp.einsum(
        "kgts,skh->tkgh", weights, value_block, preferred_element_type=jnp.float32
    ).astype(jnp.bfloat16)
    return (probability, weights, attended)


def attend_backward(
    queries, key_block, value_block, probability, weights, grad_attended, score_scale
):
    grad_weights = jnp.einsum(
        "tkgh,skh->kgts", grad_attended, value_block, preferred_element_type=jnp.float32
    )
    inner = jnp.sum(probability * grad_weights, axis=-1, keepdims=True)
    grad_scores = (probability * (grad_weights - inner)).astype(jnp.bfloat16)
    grad_query_part = (
        jnp.einsum("kgts,skh->tkgh", grad_scores, key_block, preferred_element_type=jnp.float32)
        * score_scale
    )
    grad_key_part = (
        jnp.einsum("kgts,tkgh->skh", grad_scores, queries, preferred_element_type=jnp.float32)
        * score_scale
    )
    grad_value_part = jnp.einsum(
        "kgts,tkgh->skh", weights, grad_attended, preferred_element_type=jnp.float32
    )
    return (grad_query_part, grad_key_part, grad_value_part)


def contract_last(left_side, right_side):
    return lax.dot_general(
        left_side, right_side, (((1,), (1,)), ((), ())), preferred_element_type=jnp.float32
    )


def contract_first(left_side, right_side):
    return lax.dot_general(
        left_side, right_side, (((0,), (0,)), ((), ())), preferred_element_type=jnp.float32
    )


def local(inputs, positions, w_query, w_key, w_value, w_out, post_gain, cotangent):
    tok_rows = inputs.shape[0]
    kv_local = w_key.shape[1] // HEAD_DIM
    group_size = w_query.shape[1] // w_key.shape[1]
    halo_count = WINDOW // tok_rows
    score_scale = (D // HEADS) ** (-0.5)
    ctx_index = lax.axis_index("ctx")
    query_first = ctx_index * tok_rows
    key_first = query_first - halo_count * tok_rows
    cosine, sine_table = rope_tables(positions, HEAD_DIM)
    full_inputs = lax.all_gather(inputs, "head", axis=1, tiled=True)
    queries = rotate(
        jnp.dot(full_inputs, w_query, preferred_element_type=jnp.float32).reshape(
            tok_rows, kv_local * group_size, HEAD_DIM
        ),
        cosine,
        sine_table,
    ).astype(jnp.bfloat16)
    keys_local = rotate(
        jnp.dot(full_inputs, w_key, preferred_element_type=jnp.float32).reshape(
            tok_rows, kv_local, HEAD_DIM
        ),
        cosine,
        sine_table,
    ).astype(jnp.bfloat16)
    values_local = jnp.dot(full_inputs, w_value, preferred_element_type=jnp.float32).astype(
        jnp.bfloat16
    )
    kv_pair = jnp.stack([keys_local.reshape(tok_rows, kv_local * HEAD_DIM), values_local])
    moving = kv_pair
    earlier = []
    for step_index in range(halo_count):
        moving = shifted(moving, "ctx", 1)
        earlier.insert(0, moving)
    extended = jnp.concatenate(earlier + [kv_pair], axis=1)
    span_rows = extended.shape[1]
    key_block = extended[0].reshape(span_rows, kv_local, HEAD_DIM)
    value_block = extended[1].reshape(span_rows, kv_local, HEAD_DIM)
    grouped = queries.reshape(tok_rows, kv_local, group_size, HEAD_DIM)
    allowed = window_mask(query_first, key_first, tok_rows, span_rows, positions, WINDOW)
    probability, weights, attended = attend_forward(
        grouped, key_block, value_block, allowed, score_scale
    )
    attended_flat = attended.reshape(tok_rows, kv_local * group_size * HEAD_DIM)
    partial_branch = jnp.dot(attended_flat, w_out, preferred_element_type=jnp.float32)
    gain_local = post_gain.astype(jnp.float32)
    branch = lax.psum_scatter(
        partial_branch.astype(jnp.bfloat16), "head", scatter_dimension=1, tiled=True
    ).astype(jnp.float32)
    squares = lax.psum(jnp.sum(branch * branch, axis=1), "head")
    inverse_norm = lax.rsqrt(squares / D + EPSILON)
    normed = branch * inverse_norm[:, None]
    hidden = (inputs.astype(jnp.float32) + normed * gain_local[None, :]).astype(jnp.bfloat16)
    scaled_grad = cotangent.astype(jnp.float32) * gain_local[None, :]
    slopes = lax.psum(jnp.sum(scaled_grad * normed, axis=1), "head")
    branch_grad = (inverse_norm[:, None] * (scaled_grad - normed * (slopes / D)[:, None])).astype(
        jnp.bfloat16
    )
    branch_grad_full = lax.all_gather(branch_grad, "head", axis=1, tiled=True)
    grad_attended = contract_last(branch_grad_full, w_out).astype(jnp.bfloat16)
    out_terms = contract_first(attended_flat, branch_grad_full)
    grad_w_out = lax.psum_scatter(
        out_terms.astype(jnp.bfloat16), "ctx", scatter_dimension=1, tiled=True
    ).astype(jnp.float32)
    grad_grouped = grad_attended.reshape(tok_rows, kv_local, group_size, HEAD_DIM)
    grad_query_part, grad_key_part, grad_value_part = attend_backward(
        grouped, key_block, value_block, probability, weights, grad_grouped, score_scale
    )
    pair_grads = jnp.stack(
        [
            grad_key_part.reshape(span_rows, kv_local * HEAD_DIM),
            grad_value_part.reshape(span_rows, kv_local * HEAD_DIM),
        ]
    )
    own_grads = pair_grads[:, halo_count * tok_rows :]

    def slot_for(distance):
        begin_row = (halo_count - distance) * tok_rows
        return pair_grads[:, begin_row : begin_row + tok_rows]

    carried = slot_for(halo_count)
    for distance in range(halo_count - 1, -1, -1):
        carried = shifted(carried.astype(jnp.bfloat16), "ctx", -1).astype(carried.dtype)
        if distance > 0:
            carried = carried + slot_for(distance)
    summed = own_grads + carried
    grad_key_rows = (
        rotate(summed[0].reshape(tok_rows, kv_local, HEAD_DIM), cosine, -sine_table)
        .astype(jnp.bfloat16)
        .reshape(tok_rows, kv_local * HEAD_DIM)
    )
    grad_value_rows = summed[1].astype(jnp.bfloat16)
    grad_query_rows = (
        rotate(
            grad_query_part.reshape(tok_rows, kv_local * group_size, HEAD_DIM), cosine, -sine_table
        )
        .astype(jnp.bfloat16)
        .reshape(tok_rows, kv_local * group_size * HEAD_DIM)
    )
    input_terms = (
        contract_last(grad_query_rows, w_query)
        + contract_last(grad_key_rows, w_key)
        + contract_last(grad_value_rows, w_value)
    )
    grad_inputs = (
        cotangent.astype(jnp.float32)
        + lax.psum_scatter(
            input_terms.astype(jnp.bfloat16), "head", scatter_dimension=1, tiled=True
        ).astype(jnp.float32)
    ).astype(jnp.bfloat16)
    grad_rows = jnp.concatenate([grad_query_rows, grad_key_rows, grad_value_rows], axis=1)
    query_cols = w_query.shape[1]
    key_cols = w_key.shape[1]
    stacked = lax.psum_scatter(
        contract_first(full_inputs, grad_rows).astype(jnp.bfloat16),
        "ctx",
        scatter_dimension=0,
        tiled=True,
    ).astype(jnp.float32)
    grad_w_query = stacked[:, :query_cols]
    grad_w_key = stacked[:, query_cols : query_cols + key_cols]
    grad_w_value = stacked[:, query_cols + key_cols :]
    return (hidden, grad_inputs, grad_w_query, grad_w_key, grad_w_value, grad_w_out)


def solution(mesh):
    in_specs = (
        P("ctx", "head"),
        P("ctx"),
        P(None, "head"),
        P(None, "head"),
        P(None, "head"),
        P("head", None),
        P("head"),
        P("ctx", "head"),
    )
    out_specs = (
        P("ctx", "head"),
        P("ctx", "head"),
        P("ctx", "head"),
        P("ctx", "head"),
        P("ctx", "head"),
        P("head", "ctx"),
    )
    return jax.shard_map(local, mesh=mesh, in_specs=in_specs, out_specs=out_specs, check_vma=False)
```

profile of v0, /device:TPU:1, one launch (start us, length us, event | category | flops | bytes accessed | tf_op | source)
XLA Modules:
  0.0 559.9 jit_solution(18153425733185148885)
XLA Ops:
  11.0 40.7 %all-gather.3.cloned.1.call-done = bf16[256,5376]{0,1:T(8,128)(2,1)} async-done(((bf16[256,336]{0,1:T(8,128)(2,1)}), bf16[256,5376]{0,1:T(8,128)(2,1)}) %all-gather.3.cloned.1.call-update) | async-done | bytes 2752528 | tf_op jit(solution)/shard_map/all_gather | solution.py:118
  51.8 3.0 convolution_bitcast_fusion.3
  56.0 3.1 collective-permute-start
  61.7 4.7 collective-permute-start.1
  67.7 4.5 collective-permute-start.2
  73.8 3.8 collective-permute-start.3
  86.8 2.8 convolution_convert_fusion.2
  90.2 86.9 %reduce-scatter.7.cloned.1.call-done = bf16[256,336]{0,1:T(8,128)(2,1)} async-done(((bf16[256,5376]{0,1:T(8,128)(2,1)}), bf16[256,336]{0,1:T(8,128)(2,1)}) %reduce-scatter.7.cloned.1.call-update) | async-done | bytes 172048 | tf_op jit(solution)/shard_map/reduce_scatter | solution.py:154
  178.1 30.6 %psum.14 = f32[256]{0:T(256)S(1)} all-reduce(f32[256]{0:T(256)S(1)} %fusion.31), channel_id=1, replica_groups=mesh['ctx'=16,'head'=16] {'head'}, use_global_device_ids=true, to_apply=%region_4.5 | all-reduce | flops 256 | bytes 2048 | tf_op jit(solution)/shard_map/psum | solution.py:157
  209.8 27.7 %psum.15 = f32[256]{0:T(256)S(1)} all-reduce(f32[256]{0:T(256)S(1)} %fusion.30), channel_id=1, replica_groups=mesh['ctx'=16,'head'=16] {'head'}, use_global_device_ids=true, to_apply=%region_6.7 | all-reduce | flops 256 | bytes 2048 | tf_op jit(solution)/shard_map/psum | solution.py:162
  239.4 36.9 %all-gather.5.cloned.1.call-done = bf16[256,5376]{0,1:T(8,128)(2,1)} async-done(((bf16[256,336]{0,1:T(8,128)(2,1)}), bf16[256,5376]{0,1:T(8,128)(2,1)}) %all-gather.5.cloned.1.call-update) | async-done | bytes 2752528 | tf_op jit(solution)/shard_map/all_gather | solution.py:166
  276.3 4.3 convolution_convert_fusion.1
  280.7 2.8 convolution_convert_fusion.3
  288.0 5.4 collective-permute-done.4
  295.6 4.0 collective-permute-done.5
  303.5 3.8 collective-permute-done.6
  309.6 2.8 fusion.89
  312.4 8.9 %collective-permute-done.7 = bf16[2,256,128]{1,2,0:T(8,128)(2,1)S(1)} collective-permute-done((bf16[2,256,128]{1,2,0:T(8,128)(2,1)S(1)}, bf16[2,256,128]{1,2,0:T(8,128)(2,1)S(1)}, u32[]{:S(2)}, u32[]{:S(2)}) %collective-permute-start.7) | collective-permute-done | bytes 131104 | tf_op jit(solution)/shard_map/ppermute | solution.py:21
  323.0 2.4 fusion.1
  326.4 5.9 %fusion = bf16[5376,512]{0,1:T(8,128)(2,1)} fusion(bf16[256,5376]{0,1:T(8,128)(2,1)} %all-gather.3.cloned.1.call-done, bf16[256,128]{0,1:T(8,128)(2,1)S(1)} %fusion.69, bf16[256,64]{0,1:T(8,128)(2,1)S(1)} %get-tuple-element.35, bf16[256,64]{0,1:T(8,128)(2,1)S(1)} %get-tuple-element.34, bf16[256,256]{0,1:T(8,128)(2,1)S(1)} %bitcast.112), kind=kOutput, calls=%fused_computation.3 | convolution fusion | flops 1413087232 | bytes 8519680 | tf_op jit(solution)/shard_map/dot_general | solution.py:103
  332.3 8.3 %copy.76 = bf16[5376,512]{1,0:T(8,128)(2,1)} copy(bf16[5376,512]{0,1:T(8,128)(2,1)} %fusion) | data formatting | bytes 11010048
  340.6 34.6 %reduce-scatter.11.cloned.1.call-done = bf16[256,336]{0,1:T(8,128)(2,1)} async-done(((bf16[256,5376]{0,1:T(8,128)(2,1)}), bf16[256,336]{0,1:T(8,128)(2,1)}) %reduce-scatter.11.cloned.1.call-update) | async-done | bytes 172048 | tf_op jit(solution)/shard_map/reduce_scatter | solution.py:169
  376.9 63.3 %reduce-scatter.9.cloned.1.call-done = bf16[256,336]{0,1:T(8,128)(2,1)} async-done(((bf16[256,5376]{0,1:T(8,128)(2,1)}), bf16[256,336]{0,1:T(8,128)(2,1)}) %reduce-scatter.9.cloned.1.call-update) | async-done | bytes 172048 | tf_op jit(solution)/shard_map/reduce_scatter | solution.py:214
  441.8 104.9 %reduce-scatter.13.cloned.1.call-done = bf16[336,512]{1,0:T(8,128)(2,1)} async-done(((bf16[5376,512]{1,0:T(8,128)(2,1)}), bf16[336,512]{1,0:T(8,128)(2,1)}) %reduce-scatter.13.cloned.1.call-update) | async-done | bytes 344080
  (128 shorter events, 49.1 us)
Async XLA Ops:
  7.2 79.6 %copy-start = (bf16[256,5376]{1,0:T(8,128)(2,1)S(1)}, bf16[256,5376]{1,0:T(8,128)(2,1)}, u32[]{:S(2)}) copy-start(bf16[256,5376]{1,0:T(8,128)(2,1)} %param.13) | copy-start | bytes 8257540
  7.2 44.6 %all-gather.3.cloned.1.call-start = ((), (), s32[]{:S(2)}) async-start(), calls=%async_computation.4 | async-start | bytes 2924544 | tf_op jit(solution)/shard_map/all_gather | solution.py:118
  7.9 169.2 %reduce-scatter.7.cloned.1.call-start = ((), (), s32[]{:S(2)}) async-start(), calls=%async_computation.5 | async-start | bytes 2924544 | tf_op jit(solution)/shard_map/reduce_scatter | solution.py:154
  54.8 11.6 %copy-start.7 = (bf16[5376,256]{1,0:T(8,128)(2,1)S(1)}, bf16[5376,256]{1,0:T(8,128)(2,1)}, u32[]{:S(2)}) copy-start(bf16[5376,256]{1,0:T(8,128)(2,1)} %param.10) | copy-start | bytes 8257540
  56.0 5.7 %collective-permute-start = (bf16[2,256,128]{1,2,0:T(8,128)(2,1)S(1)}, bf16[2,256,128]{1,2,0:T(8,128)(2,1)S(1)}, u32[]{:S(2)}, u32[]{:S(2)}) collective-permute-start(bf16[2,256,128]{1,2,0:T(8,128)(2,1)S(1)} %pad_maximum_fusion.1), channel_id=1, source_target_pairs={{0,16},{16,32},{32,48},{48,64},{64,80},{80,96},{96,112},{112,128},... | collective-permute-start | bytes 393224 | tf_op jit(solution)/shard_map/ppermute | solution.py:21
  61.7 6.0 %collective-permute-start.1 = (bf16[2,256,128]{1,2,0:T(8,128)(2,1)S(1)}, bf16[2,256,128]{1,2,0:T(8,128)(2,1)}, u32[]{:S(2)}, u32[]{:S(2)}) collective-permute-start(bf16[2,256,128]{1,2,0:T(8,128)(2,1)S(1)} %collective-permute-done), channel_id=1, source_target_pairs={{0,16},{16,32},{32,48},{48,64},{64,80},{80,96},{96,112},{112,128},... | collective-permute-start | bytes 393224 | tf_op jit(solution)/shard_map/ppermute | solution.py:21
  67.7 6.1 %collective-permute-start.2 = (bf16[2,256,128]{1,2,0:T(8,128)(2,1)}, bf16[2,256,128]{1,2,0:T(8,128)(2,1)}, u32[]{:S(2)}, u32[]{:S(2)}) collective-permute-start(bf16[2,256,128]{1,2,0:T(8,128)(2,1)} %collective-permute-done.1), channel_id=1, source_target_pairs={{0,16},{16,32},{32,48},{48,64},{64,80},{80,96},{96,112},{112,128},... | collective-permute-start | bytes 393224 | tf_op jit(solution)/shard_map/ppermute | solution.py:21
  73.8 6.0 %collective-permute-start.3 = (bf16[2,256,128]{1,2,0:T(8,128)(2,1)}, bf16[2,256,128]{1,2,0:T(8,128)(2,1)S(1)}, u32[]{:S(2)}, u32[]{:S(2)}) collective-permute-start(bf16[2,256,128]{1,2,0:T(8,128)(2,1)} %collective-permute-done.2), channel_id=1, source_target_pairs={{0,16},{16,32},{32,48},{48,64},{64,80},{80,96},{96,112},{112,128},... | collective-permute-start | bytes 393224 | tf_op jit(solution)/shard_map/ppermute | solution.py:21
  89.6 119.2 %copy-start.8 = (bf16[256,336]{0,1:T(8,128)(2,1)S(1)}, bf16[256,336]{0,1:T(8,128)(2,1)}, u32[]{:S(2)}) copy-start(bf16[256,336]{0,1:T(8,128)(2,1)} %param.15) | copy-start | bytes 516100
  89.6 148.0 %copy-start.13 = (bf16[256,336]{0,1:T(8,128)(2,1)S(1)}, bf16[256,336]{0,1:T(8,128)(2,1)}, u32[]{:S(2)}) copy-start(bf16[256,336]{0,1:T(8,128)(2,1)} %param.8) | copy-start | bytes 516100
  89.6 186.7 %all-gather.5.cloned.1.call-start = ((), (), s32[]{:S(2)}) async-start(), calls=%async_computation.6 | async-start | bytes 2924544 | tf_op jit(solution)/shard_map/all_gather | solution.py:166
  239.4 135.9 %reduce-scatter.11.cloned.1.call-start = ((), (), s32[]{:S(2)}) async-start(), calls=%async_computation.8 | async-start | bytes 2924544 | tf_op jit(solution)/shard_map/reduce_scatter | solution.py:169
  280.7 159.5 %reduce-scatter.9.cloned.1.call-start = ((), (), s32[]{:S(2)}) async-start(), calls=%async_computation.7 | async-start | bytes 2924544 | tf_op jit(solution)/shard_map/reduce_scatter | solution.py:214
  286.5 13.7 %copy-start.1 = (f32[1,1280,128]{1,2,0:T(8,128)}, f32[1,1280,128]{1,2,0:T(8,128)S(1)}, u32[]{:S(2)}) copy-start(f32[1,1280,128]{1,2,0:T(8,128)S(1)} %convolution_bitcast_fusion.1) | copy-start | bytes 1966084
  286.5 8.4 %copy-start.21 = (bf16[2,1280,128]{1,2,0:T(8,128)(2,1)S(1)}, bf16[2,1280,128]{1,2,0:T(8,128)(2,1)}, u32[]{:S(2)}) copy-start(bf16[2,1280,128]{1,2,0:T(8,128)(2,1)} %copy-done.19) | copy-start | bytes 1966084
  286.6 15.0 %copy-start.18 = (f32[256,64]{1,0:T(8,128)S(1)}, f32[256,64]{1,0:T(8,128)}, u32[]{:S(2)}) copy-start(f32[256,64]{1,0:T(8,128)} %get-tuple-element.38) | copy-start | bytes 196612
  286.6 6.9 %collective-permute-start.4 = (bf16[2,256,128]{1,2,0:T(8,128)(2,1)S(1)}, bf16[2,256,128]{1,2,0:T(8,128)(2,1)S(1)}, u32[]{:S(2)}, u32[]{:S(2)}) collective-permute-start(bf16[2,256,128]{1,2,0:T(8,128)(2,1)S(1)} %fusion.39), channel_id=1, source_target_pairs={{16,0},{32,16},{48,32},{64,48},{80,64},{96,80},{112,96},{128,112},... | collective-permute-start | bytes 393224 | tf_op jit(solution)/shard_map/ppermute | solution.py:21
  293.5 6.1 %collective-permute-start.5 = (bf16[2,256,128]{1,2,0:T(8,128)(2,1)S(1)}, bf16[2,256,128]{1,2,0:T(8,128)(2,1)S(1)}, u32[]{:S(2)}, u32[]{:S(2)}) collective-permute-start(bf16[2,256,128]{1,2,0:T(8,128)(2,1)S(1)} %fusion.42), channel_id=1, source_target_pairs={{16,0},{32,16},{48,32},{64,48},{80,64},{96,80},{112,96},{128,112},... | collective-permute-start | bytes 393224 | tf_op jit(solution)/shard_map/ppermute | solution.py:21
  300.2 7.0 %collective-permute-start.6 = (bf16[2,256,128]{1,2,0:T(8,128)(2,1)}, bf16[2,256,128]{1,2,0:T(8,128)(2,1)}, u32[]{:S(2)}, u32[]{:S(2)}) collective-permute-start(bf16[2,256,128]{1,2,0:T(8,128)(2,1)} %fusion.35), channel_id=1, source_target_pairs={{16,0},{32,16},{48,32},{64,48},{80,64},{96,80},{112,96},{128,112},... | collective-permute-start | bytes 393224 | tf_op jit(solution)/shard_map/ppermute | solution.py:21
  308.3 13.0 %collective-permute-start.7 = (bf16[2,256,128]{1,2,0:T(8,128)(2,1)S(1)}, bf16[2,256,128]{1,2,0:T(8,128)(2,1)S(1)}, u32[]{:S(2)}, u32[]{:S(2)}) collective-permute-start(bf16[2,256,128]{1,2,0:T(8,128)(2,1)S(1)} %fusion.44), channel_id=1, source_target_pairs={{16,0},{32,16},{48,32},{64,48},{80,64},{96,80},{112,96},{128,112},... | collective-permute-start | bytes 393224 | tf_op jit(solution)/shard_map/ppermute | solution.py:21
  309.6 11.7 %copy-start.2 = (f32[1,1280,128]{1,2,0:T(8,128)S(1)}, f32[1,1280,128]{1,2,0:T(8,128)}, u32[]{:S(2)}) copy-start(f32[1,1280,128]{1,2,0:T(8,128)} %copy-done.1) | copy-start | bytes 1966084
  312.3 9.3 %copy-start.6 = (bf16[5376,128]{1,0:T(8,128)(2,1)S(1)}, bf16[5376,128]{1,0:T(8,128)(2,1)}, u32[]{:S(2)}) copy-start(bf16[5376,128]{1,0:T(8,128)(2,1)} %param.11) | copy-start | bytes 4128772
  325.4 221.3 %reduce-scatter.13.cloned.1.call-start = ((), (), s32[]{:S(2)}) async-start(), calls=%async_computation.9 | async-start | bytes 5849088
  340.6 99.6 %copy-start.9 = (bf16[256,336]{0,1:T(8,128)(2,1)S(1)}, bf16[256,336]{0,1:T(8,128)(2,1)}, u32[]{:S(2)}) copy-start(bf16[256,336]{0,1:T(8,128)(2,1)} %param.15) | copy-start | bytes 516100
  (17 other events, 49.7 us)
Sparse Core Ops, SparseCore 0:
  9.9 41.8 all-gather.2
  89.7 87.3 reduce-scatter.6
  239.5 36.8 all-gather.4
  280.8 94.4 reduce-scatter.10
  377.8 62.3 reduce-scatter.8
  443.7 102.9 reduce-scatter.12
where the time goes:
time: 562 us; the launch traced here: 560 us
  waiting for transfers between devices  394 us (70%)
  blocking collectives  58.3 us (10%)
  matrix products  31.8 us (6%)
  starting transfers between devices  21.9 us (4%)
  local copies, waits for them, and re-layouts  21.7 us (4%)
  other arithmetic  17.6 us (3%)
  between operations  14.6 us (3%)
    unnamed x7, waiting for transfers between devices  106 us
    reduce_scatter x1, waiting for transfers between devices, local(): lax.psum_scatter(partial_branch.astype(jnp.bfloat16), 'head', scatter_dim...  86.9 us
    reduce_scatter x1, waiting for transfers between devices, local(): lax.psum_scatter(input_terms.astype(jnp.bfloat16), 'head', scatter_dimens...  63.3 us
    all_gather x1, waiting for transfers between devices, local(): full_inputs = lax.all_gather(inputs, 'head', axis=1, tiled=True)  40.7 us
    all_gather x1, waiting for transfers between devices, local(): branch_grad_full = lax.all_gather(branch_grad, 'head', axis=1, tiled=True)  36.9 us
    reduce_scatter x1, waiting for transfers between devices, local(): lax.psum_scatter(out_terms.astype(jnp.bfloat16), 'ctx', scatter_dimension...  34.6 us
    psum x1, blocking collectives, local(): squares = lax.psum(jnp.sum(branch * branch, axis=1), 'head')  30.6 us
    psum x1, blocking collectives, local(): slopes = lax.psum(jnp.sum(scaled_grad * normed, axis=1), 'head')  27.7 us
  transfers between devices with their start and end apart: 14, of which 13 were waited for; matrix products, arithmetic and copies ran while one was open for 7% of the time, Pallas kernels for 0%

commit v1 on v0

v1 whole, which is shorter than its diff:
```python
import functools
import math

import jax
import jax.numpy as jnp
from jax import lax
from jax.experimental import pallas as pl
from jax.experimental.pallas import tpu as pltpu
from jax.sharding import PartitionSpec as P

D = 5376
HEADS = 32
WINDOW = 1024
EPSILON = 1e-06
ROPE_BASE = 10000.0
HD = 128
T = 256
BLK = 336
PAIR = 672
MESH = pl.DeviceIdType.MESH
F32 = jnp.float32
BF16 = jnp.bfloat16
SCALE = (D // HEADS) ** (-0.5)
STEP = 32


def dot_nn(a, b):
    return lax.dot_general(a, b, (((1,), (0,)), ((), ())), preferred_element_type=F32)


def dot_nt(a, b):
    return lax.dot_general(a, b, (((1,), (1,)), ((), ())), preferred_element_type=F32)


def dot_tn(a, b):
    return lax.dot_general(a, b, (((0,), (0,)), ((), ())), preferred_element_type=F32)


def rot(v, cos, sin):
    half = HD // 2
    a, b = v[:half], v[half:]
    return jnp.concatenate([a * cos - b * sin, b * cos + a * sin], axis=0)


def fold(v):
    total = v[0:8]
    for i in range(8, v.shape[0], 8):
        total = total + v[i : i + 8]
    return total


def kernel(
    x_ref, cot_ref, pos_ref, cos_ref, sin_ref, gain_ref, wq_hbm, wk_hbm, wv_hbm, wo_hbm,
    hidden_ref, gin_ref, dwq_ref, dwk_ref, dwv_ref, dwo_ref,
    w, wo, wot, xt, xa, part, bg, bgt, att_all, att, qt, ga, kv, s_scr, p_scr, wt_scr, g_all,
    acc, r_core, r_x, r_x2, r_z, s_buf, branch, stat, halo_out, halo_in, halo_prev, halo_z, dw_out, dw_in,
    load_sem, ag_s, ag_r, rs_s, rs_r, st_s, st_r, kv_s, kv_r, xa_s, xa_r, at_s, at_r, pm_s, pm_r,
    ha_s, ha_r, g_s, g_r, dw_s, dw_r,
):
    c = lax.axis_index("ctx")
    h = lax.axis_index("head")
    zh, y = c // 4, c % 4
    zl, x, q = h // 8, (h // 2) % 4, h % 2

    def head_of(o):
        return ((zl + o[0]) % 2) * 8 + ((x + o[1]) % 4) * 2 + (q + o[2]) % 2

    def at_head(o):
        return (c, head_of(o))

    def at_y(r):
        return (zh * 4 + (y + r) % 4, h)

    def at_z(r):
        return (((zh + r) % 4) * 4 + y, h)

    def rows(index, size=BLK):
        return pl.ds(pl.multiple_of(index * size, 16), size)

    pending = []

    def push(src, dst, ssem, rsem, device):
        copy = pltpu.make_async_remote_copy(
            src_ref=src, dst_ref=dst, send_sem=ssem, recv_sem=rsem, device_id=device, device_id_type=MESH
        )
        copy.start()
        return copy

    def send(*args):
        pending.append(push(*args))

    def landed(dst, ssem, rsem):
        pltpu.make_async_remote_copy(
            src_ref=dst, dst_ref=dst, send_sem=ssem, recv_sem=rsem, device_id=at_y(1), device_id_type=MESH
        ).wait_recv()

    loads = []
    for i, (src, dst) in enumerate(
        (
            (wq_hbm, w.at[:, 0:256]),
            (wk_hbm, w.at[:, 256:384]),
            (wv_hbm, w.at[:, 384:512]),
            (wo_hbm, wo),
        )
    ):
        cp = pltpu.make_async_copy(src, dst, load_sem.at[i])
        cp.start()
        loads.append(cp)
    xt[rows(h), :] = x_ref[...]

    barrier = pltpu.get_barrier_semaphore()
    others = [(a, b, d) for a in (0, 1) for b in range(4) for d in (0, 1) if (a, b, d) != (0, 0, 0)]
    for o in others:
        pl.semaphore_signal(barrier, inc=1, device_id=at_head(o), device_id_type=MESH)
    for r in (1, 2, 3):
        pl.semaphore_signal(barrier, inc=1, device_id=at_y(r), device_id_type=MESH)
        pl.semaphore_signal(barrier, inc=1, device_id=at_z(r), device_id_type=MESH)

    @pl.when(c != h)
    def _():
        pl.semaphore_signal(barrier, inc=1, device_id=(h, c), device_id_type=MESH)
        pl.semaphore_wait(barrier, 22)

    @pl.when(c == h)
    def _():
        pl.semaphore_wait(barrier, 21)

    def gather(buf, ss, rs):
        def key(o):
            return o[0] * 8 + o[1] * 2 + o[2]

        def forward(o, e):
            rel = ((o[0] + e[0]) % 2, (o[1] - e[1]) % 4, (o[2] + e[2]) % 2)
            block = buf.at[rows(head_of(o)), :]
            send(block, block, ss.at[key(rel)], rs.at[key(rel)], at_head(e))

        def wait(o):
            block = buf.at[rows(head_of(o)), :]
            landed(block, ss.at[key(o)], rs.at[key(o)])

        def begin():
            for e in ((1, 0, 0), (0, 1, 0), (0, 3, 0), (0, 2, 0), (0, 0, 1)):
                forward((0, 0, 0), e)

        events = (
            ((1, 0), ((0, 1, 0), (0, 3, 0), (0, 0, 1))),
            ((0, 1), ((0, 0, 1),)),
            ((0, 3), ((0, 0, 1),)),
            ((0, 2), ((1, 0, 0), (0, 0, 1))),
            ((1, 1), ((0, 0, 1),)),
            ((1, 3), ((0, 0, 1),)),
            ((1, 2), ((0, 0, 1),)),
        )

        def finish(consume):
            def take(chip):
                wait((chip[0], chip[1], 1))
                consume(head_of((chip[0], chip[1], 0)) // 2)

            last = (0, 0)
            for chip, targets in events:
                wait((chip[0], chip[1], 0))
                for e in targets:
                    forward((chip[0], chip[1], 0), e)
                take(last)
                last = chip
            take(last)

        return begin, finish

    def scatter(produce, k):
        ss, rs = rs_s.at[k], rs_r.at[k]
        rc, rx, rx2, rz, sb, pt = r_core.at[k], r_x.at[k], r_x2.at[k], r_z.at[k], s_buf.at[k], part.at[k]
        order = ((1, 2), (1, 1), (1, 3), (0, 1), (0, 3), (0, 2), (1, 0), (0, 0))

        def make(i):
            chip = head_of((order[i][0], order[i][1], 0)) // 2
            pt[rows(chip, PAIR), :] = produce(chip).astype(BF16)
            block = pt.at[rows(chip * 2 + 1 - q), :]
            send(block, rc.at[i], ss.at[i], rs.at[i], at_head((0, 0, 1)))

        def settle(i):
            dz, dx = order[i]
            landed(rc.at[i], ss.at[i], rs.at[i])
            total = pt[rows(head_of((dz, dx, 0))), :].astype(F32) + rc[i].astype(F32)
            if (dz, dx) == (1, 2):
                sb[i] = total.astype(BF16)
                send(sb.at[i], rz.at[0], ss.at[8], rs.at[8], at_head((1, 0, 0)))
            elif dx in (1, 3):
                j = (dx // 2) * 2 + dz
                sb[i] = total.astype(BF16)
                send(sb.at[i], rx.at[j], ss.at[9 + j], rs.at[9 + j], at_head((0, dx, 0)))
            elif (dz, dx) == (0, 2):
                landed(rz.at[0], ss.at[8], rs.at[8])
                sb[i] = (total + rz[0].astype(F32)).astype(BF16)
                send(sb.at[i], rx2, ss.at[13], rs.at[13], at_head((0, 2, 0)))
            elif (dz, dx) == (1, 0):
                for j in (1, 3):
                    landed(rx.at[j], ss.at[9 + j], rs.at[9 + j])
                    total = total + rx[j].astype(F32)
                sb[i] = total.astype(BF16)
                send(sb.at[i], rz.at[1], ss.at[14], rs.at[14], at_head((1, 0, 0)))
            else:
                for j in (0, 2):
                    landed(rx.at[j], ss.at[9 + j], rs.at[9 + j])
                    total = total + rx[j].astype(F32)
                landed(rx2, ss.at[13], rs.at[13])
                total = total + rx2[...].astype(F32)
                landed(rz.at[1], ss.at[14], rs.at[14])
                total = total + rz[1].astype(F32)
                return total
            return None

        for i in range(8):
            make(i)
            if i > 0:
                settle(i - 1)
        return settle(7)

    ag_begin, ag_finish = gather(xt, ag_s.at[0], ag_r.at[0])
    ag_begin()
    acc[...] = jnp.zeros_like(acc)
    loads[3].wait()

    def turn(i, carry):
        at = pl.multiple_of(i * 128, 128)
        wot[pl.ds(at, 128), :] = wo[:, pl.ds(at, 128)].T
        return carry

    lax.fori_loop(0, D // 128, turn, 0)
    for cp in loads[:3]:
        cp.wait()

    def project(chip):
        acc[...] += dot_tn(w[rows(chip, PAIR), :], xt[rows(chip, PAIR), :])

    ag_finish(project)
    cos, sin = cos_ref[...], sin_ref[...]
    qt[:, 0:T] = rot(acc[0:128, :], cos, sin).astype(BF16)
    qt[:, T : 2 * T] = rot(acc[128:256, :], cos, sin).astype(BF16)
    kv[4, 0:128, :] = rot(acc[256:384, :], cos, sin).astype(BF16)
    kv[4, 128:256, :] = acc[384:512, :].astype(BF16)

    def kv_out(slot, r):
        return pltpu.make_async_remote_copy(
            src_ref=kv.at[slot], dst_ref=kv.at[4 - r], send_sem=kv_s.at[r], recv_sem=kv_r.at[r],
            device_id=at_y(r), device_id_type=MESH,
        )

    def kv_up():
        return pltpu.make_async_remote_copy(
            src_ref=kv.at[4], dst_ref=kv.at[0], send_sem=kv_s.at[0], recv_sem=kv_r.at[0],
            device_id=at_z(1), device_id_type=MESH,
        )

    @pl.when(zh < 3)
    def _():
        kv_up().start()

    for r in (1, 2, 3):

        @pl.when(y + r < 4)
        def _():
            kv_out(4, r).start()

    @pl.when(zh == 0)
    def _():
        kv[0] = jnp.zeros((256, T), BF16)

    @pl.when(zh > 0)
    def _():
        kv_up().wait_recv()

    for r in (1, 2, 3):

        @pl.when(y + r >= 4)
        def _():
            kv_out(0, r).start()

    lane = lax.broadcasted_iota(jnp.int32, (1, T), 1)
    limit = jnp.minimum(jnp.minimum(pos_ref[...], WINDOW - 1), lane + c * T)
    limit = jnp.concatenate([limit, limit], axis=1)
    token = jnp.concatenate([lane, lane], axis=1)
    base = lax.broadcasted_iota(jnp.int32, (STEP, 2 * T), 0)
    gap = token - base
    neg = jnp.full((STEP, 2 * T), -jnp.inf, F32)

    highest = jnp.full((8, 2 * T), -jnp.inf, F32)
    for slot in (4, 0, 3, 1, 2):
        if slot in (1, 2, 3):
            kv_out(0, 4 - slot).wait_recv()
        s_scr[slot] = dot_tn(kv[slot, 0:128, :], qt[...])

        def mask(i, top, slot=slot):
            at = pl.multiple_of(i * STEP, STEP)
            distance = gap + ((4 - slot) * T - at)
            scores = s_scr[slot, pl.ds(at, STEP), :] * SCALE
            scores = jnp.where((distance >= 0) & (distance <= limit), scores, neg)
            s_scr[slot, pl.ds(at, STEP), :] = scores
            for j in range(0, STEP, 8):
                top = jnp.maximum(top, scores[j : j + 8])
            return top

        highest = lax.fori_loop(0, T // STEP, mask, highest)
    highest = jnp.max(highest, axis=0, keepdims=True)

    def expo(i, total):
        at = pl.multiple_of(i * STEP, STEP)
        slot, at = i // (T // STEP), pl.multiple_of((i % (T // STEP)) * STEP, STEP)
        e = jnp.exp(s_scr[slot, pl.ds(at, STEP), :] - highest)
        p_scr[slot, pl.ds(at, STEP), :] = e
        return total + fold(e)

    total = lax.fori_loop(0, 5 * T // STEP, expo, jnp.zeros((8, 2 * T), F32))
    recip = 1.0 / jnp.sum(total, axis=0, keepdims=True)

    def norm(i, carry):
        slot, at = i // (T // STEP), pl.multiple_of((i % (T // STEP)) * STEP, STEP)
        p = p_scr[slot, pl.ds(at, STEP), :] * recip
        p_scr[slot, pl.ds(at, STEP), :] = p
        wt_scr[slot, pl.ds(at, STEP), :] = p.astype(BF16)
        return carry

    lax.fori_loop(0, 5 * T // STEP, norm, 0)
    out = dot_nn(kv[0, 128:256, :], wt_scr[0])
    for slot in range(1, 5):
        out = out + dot_nn(kv[slot, 128:256, :], wt_scr[slot])
    out = out.astype(BF16)
    att[0:128, :] = out[:, 0:T]
    att[128:256, :] = out[:, T : 2 * T]
    att_all[c] = att[...]

    for r in (1, 2, 3):
        send(att, att_all.at[c], at_s.at[r], at_r.at[r], at_z(r))

    def project_out(chip):
        return dot_nn(wot[rows(chip, PAIR), :], att[...])

    branch[...] = scatter(project_out, 0)
    gain = gain_ref[...]
    scaled = cot_ref[...].astype(F32) * gain
    stat[h] = jnp.zeros((8, T), F32)
    stat[h, 0:1, :] = jnp.sum(branch[...] * branch[...], axis=0, keepdims=True)
    stat[h, 1:2, :] = jnp.sum(scaled * branch[...], axis=0, keepdims=True)
    for i, o in enumerate(others):
        send(stat.at[h], stat.at[h], st_s.at[i], st_r.at[i], at_head(o))

    for r in (1, 2, 3):
        source = ((zh + 4 - r) % 4) * 4 + y
        landed(att_all.at[source], at_s.at[r], at_r.at[r])
    for r in (1, 2, 3):
        for dz in range(4):
            block = att_all.at[((zh + dz) % 4) * 4 + y]
            i = 4 + (r - 1) * 4 + dz
            send(block, block, at_s.at[i], at_r.at[i], at_y(r))

    for i, o in enumerate(others):
        back = head_of((o[0], (4 - o[1]) % 4, o[2]))
        landed(stat.at[back], st_s.at[i], st_r.at[i])
    sums = stat[0]
    for i in range(1, 16):
        sums = sums + stat[i]
    inverse = lax.rsqrt(sums[0:1] / D + EPSILON)
    slopes = inverse * sums[1:2] / D
    normed = branch[...] * inverse
    bg[rows(h), :] = (inverse * (scaled - normed * slopes)).astype(BF16)
    bg_begin, bg_finish = gather(bg, ag_s.at[1], ag_r.at[1])
    bg_begin()
    hidden_ref[...] = (x_ref[...].astype(F32) + normed * gain).astype(BF16)

    def mirror():
        return pltpu.make_async_remote_copy(
            src_ref=bg.at[rows(h), :], dst_ref=bgt.at[rows(c), :], send_sem=pm_s, recv_sem=pm_r,
            device_id=(h, c), device_id_type=MESH,
        )

    def mirrored():
        return pltpu.make_async_remote_copy(
            src_ref=bg.at[rows(h), :], dst_ref=bgt.at[rows(h), :], send_sem=pm_s, recv_sem=pm_r,
            device_id=(h, c), device_id_type=MESH,
        )

    @pl.when(c != h)
    def _():
        mirror().start()

    @pl.when(c == h)
    def _():
        bgt[rows(h), :] = bg[rows(h), :]

    for r in (1, 2, 3):
        for dz in range(4):
            i = (r - 1) * 4 + dz
            send(
                xt.at[rows(dz * 4 + (y + r) % 4), :], xa.at[r - 1, dz], xa_s.at[i], xa_r.at[i], at_y(r)
            )

    acc[0:256, :] = jnp.zeros((256, T), F32)

    def project_back(chip):
        acc[0:256, :] += dot_tn(wot[rows(chip, PAIR), :], bg[rows(chip, PAIR), :])

    bg_finish(project_back)
    ga[:, 0:T] = acc[0:128, :].astype(BF16)
    ga[:, T : 2 * T] = acc[128:256, :].astype(BF16)

    @pl.when(c != h)
    def _():
        mirrored().wait_recv()

    bgt_begin, bgt_finish = gather(bgt, ag_s.at[2], ag_r.at[2])
    bgt_begin()

    inner = jnp.zeros((8, 2 * T), F32)
    for slot in range(5):
        s_scr[slot] = dot_tn(kv[slot, 128:256, :], ga[...])

    def weigh(i, total):
        slot, at = i // (T // STEP), pl.multiple_of((i % (T // STEP)) * STEP, STEP)
        return total + fold(p_scr[slot, pl.ds(at, STEP), :] * s_scr[slot, pl.ds(at, STEP), :])

    inner = jnp.sum(lax.fori_loop(0, 5 * T // STEP, weigh, inner), axis=0, keepdims=True)

    ds = acc_ds = None
    dq = None
    own_kv = None
    for slot in (1, 2, 3, 0, 4):

        def grad(i, carry, slot=slot):
            at = pl.multiple_of(i * STEP, STEP)
            p = p_scr[slot, pl.ds(at, STEP), :]
            d = p * (s_scr[slot, pl.ds(at, STEP), :] - inner)
            part[1, pl.ds(pl.multiple_of(slot * 512 + at, STEP), STEP), :] = d[:, 0:T].astype(BF16)
            part[1, pl.ds(pl.multiple_of(slot * 512 + 256 + at, STEP), STEP), :] = d[:, T : 2 * T].astype(BF16)
            return carry

        lax.fori_loop(0, T // STEP, grad, 0)
        d0 = part[1, slot * 512 : slot * 512 + 256, :]
        d1 = part[1, slot * 512 + 256 : slot * 512 + 512, :]
        dk = (dot_nt(qt[:, 0:T], d0) + dot_nt(qt[:, T : 2 * T], d1)) * SCALE
        dv = dot_nt(ga[...], wt_scr[slot])
        if slot in (1, 2, 3):
            halo_out[slot - 1, 0:128, :] = dk.astype(BF16)
            halo_out[slot - 1, 128:256, :] = dv.astype(BF16)
            send(
                halo_out.at[slot - 1], halo_in.at[slot - 1], ha_s.at[slot], ha_r.at[slot], at_y(slot)
            )
        else:
            i = 0 if slot == 0 else 1
            halo_prev[i, 0:128, :] = dk
            halo_prev[i, 128:256, :] = dv
        k_slot = kv[slot, 0:128, :]
        part0, part1 = dot_nn(k_slot, d0), dot_nn(k_slot, d1)
        if dq is None:
            acc[0:128, :] = part0
            acc[128:256, :] = part1
            dq = True
        else:
            acc[0:128, :] += part0
            acc[128:256, :] += part1

    g_all[0, 0:128, :] = rot(acc[0:128, :] * SCALE, cos, -sin).astype(BF16)
    g_all[0, 128:256, :] = rot(acc[128:256, :] * SCALE, cos, -sin).astype(BF16)
    for r in (1, 2, 3):
        send(
            g_all.at[0, 0:256, :], g_all.at[r, 0:256, :], g_s.at[r - 1], g_r.at[r - 1], at_y(r)
        )

    for r in (1, 2, 3):
        landed(halo_in.at[r - 1], ha_s.at[r], ha_r.at[r])
        value = halo_in[r - 1].astype(F32)
        back = (y >= r).astype(F32)
        halo_prev[0] += value * back
        halo_prev[1] += value * (1.0 - back)
    halo_z[0] = halo_prev[0].astype(BF16)

    def down():
        return pltpu.make_async_remote_copy(
            src_ref=halo_z.at[0], dst_ref=halo_z.at[1], send_sem=ha_s.at[0], recv_sem=ha_r.at[0],
            device_id=at_z(3), device_id_type=MESH,
        )

    @pl.when(zh > 0)
    def _():
        down().start()

    @pl.when(zh < 3)
    def _():
        down().wait_recv()
        halo_prev[1] += halo_z[1].astype(F32)

    g_all[0, 256:384, :] = rot(halo_prev[1, 0:128, :], cos, -sin).astype(BF16)
    g_all[0, 384:512, :] = halo_prev[1, 128:256, :].astype(BF16)
    for r in (1, 2, 3):
        send(
            g_all.at[0, 256:512, :], g_all.at[r, 256:512, :], g_s.at[r + 2], g_r.at[r + 2], at_y(r)
        )

    for r in (1, 2, 3):
        for dz in range(4):
            i = (r - 1) * 4 + dz
            landed(xa.at[r - 1, dz], xa_s.at[i], xa_r.at[i])

    def weight_grads(k):
        lo = k * 256
        for r in (1, 2, 3):
            i = r - 1 + 3 * k
            landed(g_all.at[r, lo : lo + 256, :], g_s.at[i], g_r.at[i])
        result = None
        for dz in (1, 2, 3, 0):
            z = (zh + dz) % 4
            total = dot_nt(xt[rows(z * 4 + y), :], g_all[0, lo : lo + 256, :])
            for r in (1, 2, 3):
                total = total + dot_nt(xa[r - 1, z], g_all[r, lo : lo + 256, :])
            if dz == 0:
                result = total
            else:
                i = k * 3 + dz - 1
                dw_out[i] = total.astype(BF16)
                send(dw_out.at[i], dw_in.at[i], dw_s.at[i], dw_r.at[i], at_z(dz))
        return result

    dwq_ref[...] = weight_grads(0)

    def input_terms(chip):
        return dot_nn(w[rows(chip, PAIR), :], g_all[0])

    dkv = weight_grads(1)
    dwk_ref[...] = dkv[:, 0:128]
    dwv_ref[...] = dkv[:, 128:256]
    gin_ref[...] = (cot_ref[...].astype(F32) + scatter(input_terms, 1)).astype(BF16)

    for r in (1, 2, 3):
        for dz in range(4):
            block = att_all.at[((zh + dz) % 4) * 4 + (y + 4 - r) % 4]
            i = 4 + (r - 1) * 4 + dz
            landed(block, at_s.at[i], at_r.at[i])
    dwo_ref[...] = jnp.zeros_like(dwo_ref)

    def out_grad(chip):
        for j in range(2):
            dwo_ref[...] += dot_nt(bgt[rows(chip * 2 + j), :], att_all[chip * 2 + j])

    bgt_finish(out_grad)

    for dz in (1, 2, 3):
        landed(dw_in.at[dz - 1], dw_s.at[dz - 1], dw_r.at[dz - 1])
        dwq_ref[...] += dw_in[dz - 1].astype(F32)
    for dz in (1, 2, 3):
        landed(dw_in.at[dz + 2], dw_s.at[dz + 2], dw_r.at[dz + 2])
        value = dw_in[dz + 2].astype(F32)
        dwk_ref[...] += value[:, 0:128]
        dwv_ref[...] += value[:, 128:256]

    for copy in pending:
        copy.wait_send()
    for r in (1, 2, 3):
        kv_out(0, r).wait_send()

    @pl.when(zh < 3)
    def _():
        kv_up().wait_send()

    @pl.when(zh > 0)
    def _():
        down().wait_send()

    @pl.when(c != h)
    def _():
        mirror().wait_send()


def local(inputs, positions, w_query, w_key, w_value, w_out, post_gain, cotangent):
    half = HD // 2
    frequency = jnp.exp(jnp.arange(half, dtype=F32) * (-2.0 * math.log(ROPE_BASE) / HD))
    angles = frequency[:, None] * positions.astype(F32)[None, :]
    vmem = pl.BlockSpec(memory_space=pltpu.VMEM)
    hbm = pl.BlockSpec(memory_space=pl.ANY)
    dma = pltpu.SemaphoreType.DMA
    scratch = [
        pltpu.VMEM((D, 512), BF16),
        pltpu.VMEM((256, D), BF16),
        pltpu.VMEM((D, 256), BF16),
        pltpu.VMEM((D, T), BF16),
        pltpu.VMEM((3, 4, BLK, T), BF16),
        pltpu.VMEM((2, D, T), BF16),
        pltpu.VMEM((D, T), BF16),
        pltpu.VMEM((D, T), BF16),
        pltpu.VMEM((16, 256, T), BF16),
        pltpu.VMEM((256, T), BF16),
        pltpu.VMEM((128, 2 * T), BF16),
        pltpu.VMEM((128, 2 * T), BF16),
        pltpu.VMEM((5, 256, T), BF16),
        pltpu.VMEM((5, T, 2 * T), F32),
        pltpu.VMEM((5, T, 2 * T), F32),
        pltpu.VMEM((5, T, 2 * T), BF16),
        pltpu.VMEM((4, 512, T), BF16),
        pltpu.VMEM((512, T), F32),
        pltpu.VMEM((2, 8, BLK, T), BF16),
        pltpu.VMEM((2, 4, BLK, T), BF16),
        pltpu.VMEM((2, BLK, T), BF16),
        pltpu.VMEM((2, 2, BLK, T), BF16),
        pltpu.VMEM((2, 8, BLK, T), BF16),
        pltpu.VMEM((BLK, T), F32),
        pltpu.VMEM((16, 8, T), F32),
        pltpu.VMEM((3, 256, T), BF16),
        pltpu.VMEM((3, 256, T), BF16),
        pltpu.VMEM((2, 256, T), F32),
        pltpu.VMEM((2, 256, T), BF16),
        pltpu.VMEM((6, BLK, T), BF16),
        pltpu.VMEM((6, BLK, T), BF16),
        dma((4,)),
        dma((3, 16)), dma((3, 16)),
        dma((2, 15)), dma((2, 15)),
        dma((15,)), dma((15,)),
        dma((4,)), dma((4,)),
        dma((12,)), dma((12,)),
        dma((16,)), dma((16,)),
        dma, dma,
        dma((4,)), dma((4,)),
        dma((6,)), dma((6,)),
        dma((6,)), dma((6,)),
    ]
    shapes = (
        jax.ShapeDtypeStruct((BLK, T), BF16),
        jax.ShapeDtypeStruct((BLK, T), BF16),
        jax.ShapeDtypeStruct((BLK, 256), F32),
        jax.ShapeDtypeStruct((BLK, 128), F32),
        jax.ShapeDtypeStruct((BLK, 128), F32),
        jax.ShapeDtypeStruct((BLK, 256), F32),
    )
    hidden, gin, dwq, dwk, dwv, dwo = pl.pallas_call(
        kernel,
        out_shape=shapes,
        in_specs=[vmem] * 6 + [hbm] * 4,
        out_specs=(vmem,) * 6,
        scratch_shapes=scratch,
        compiler_params=pltpu.CompilerParams(
            collective_id=0, has_side_effects=True, vmem_limit_bytes=60 * 1024 * 1024
        ),
        name="layer",
    )(
        inputs.T, cotangent.T, positions[None, :], jnp.cos(angles), jnp.sin(angles),
        post_gain.astype(F32)[:, None], w_query, w_key, w_value, w_out,
    )
    return hidden.T, gin.T, dwq, dwk, dwv, dwo.T


def solution(mesh):
    in_specs = (
        P("ctx", "head"), P("ctx"), P(None, "head"), P(None, "head"),
        P(None, "head"), P("head", None), P("head"), P("ctx", "head"),
    )
    out_specs = (P("ctx", "head"),) * 5 + (P("head", "ctx"),)
    return jax.shard_map(local, mesh=mesh, in_specs=in_specs, out_specs=out_specs, check_vma=False)
```

time: 562 us -> 211 us (0.38)
  waiting for transfers between devices: 394 us -> 0 us
  Pallas kernels: 0 us -> 194 us
  blocking collectives: 58.3 us -> 0 us
  matrix products: 31.8 us -> 0 us
  starting transfers between devices: 21.9 us -> 0 us
  other arithmetic: 17.6 us -> 1.66 us
  between operations: 14.6 us -> 0.65 us
  local copies, waits for them, and re-layouts: 21.7 us -> 11.3 us
    pallas_call x0 -> x1, Pallas kernels: none -> 194 us  [local(): pl.pallas_call(kernel, out_shape=shapes, in_specs=[vmem] * 6 + [hbm] * 4,...]
    reduce_scatter x3 -> x0, waiting for transfers between devices: 185 us -> none  [the longest x1 86.9 us: local(): lax.psum_scatter(partial_branch.astype(jnp.bfloat16), 'head', scatter_dim...]
    unnamed x7 -> x0, waiting for transfers between devices: 106 us -> none
    all_gather x2 -> x0, waiting for transfers between devices: 77.7 us -> none  [the longest x1 40.7 us: local(): full_inputs = lax.all_gather(inputs, 'head', axis=1, tiled=True)]
    psum x2 -> x0, blocking collectives: 58.3 us -> none  [the longest x1 30.6 us: local(): squares = lax.psum(jnp.sum(branch * branch, axis=1), 'head')]
    dot_general x16 -> x0, matrix products: 31.8 us -> none  [the longest x2 10.2 us: contract_first(): lax.dot_general(left_side, right_side, (((0,), (0,)), ((), ())), preferre...]
    ppermute x8 -> x0, waiting for transfers between devices: 26 us -> none  [shifted(): lax.ppermute(value, axis, [(source, source + steps) for source in range(f...]
    ppermute x8 -> x0, starting transfers between devices: 21.6 us -> none  [shifted(): lax.ppermute(value, axis, [(source, source + steps) for source in range(f...]
  transfers between devices with their start and end apart: 14 -> 0, of which waited for: 13 -> 0; matrix products, arithmetic and copies ran while one was open for 7% -> 0% of each run, Pallas kernels for 0% -> 0%
where the time goes in v1:
time: 211 us; the launch traced here: 208 us
  Pallas kernels  194 us (92%)
  local copies, waits for them, and re-layouts  11.3 us (5%)
    pallas_call x1, Pallas kernels, local(): pl.pallas_call(kernel, out_shape=shapes, in_specs=[vmem] * 6 + [hbm] * 4,...  194 us
    unnamed x6, local copies, waits for them, and re-layouts  9.85 us

profile of v1, /device:TPU:1, one launch (start us, length us, event | category | flops | bytes accessed | tf_op | source)
XLA Modules:
  0.0 207.5 jit_solution(2779670983633096727)
XLA Ops:
  0.6 0.7 convert_element_type.4
  1.3 1.0 multiply_sine_fusion
  2.3 1.5 reshape.19.gain_ref
  3.8 193.9 %layer.1 = (bf16[336,256]{1,0:T(8,128)(2,1)}, bf16[336,256]{1,0:T(8,128)(2,1)}, f32[336,256]{1,0:T(8,128)}, f32[336,128]{1,0:T(8,128)}, f32[336,128]{1,0:T(8,128)}, /*index=5*/f32[336,256]{1,0:T(8,128)}) custom-call(bf16[336,256]{1,0:T(8,128)(2,1)} %bitcast.9, bf16[336,256]{1,0:T(8,128)(2,1)} %bitcast.10, s32[1,256]{1,0:T(1,128)} %bitcast.11, ...), custom_call_target="tpu_custom_call" | custom-call | tf_op jit(solution)/shard_map/layer/pallas_call | solution.py:632
  197.7 1.6 copy.21
  199.3 1.6 copy.22
  200.9 1.7 copy.23
  202.6 1.6 copy.24
  204.2 1.6 copy.25
  205.8 1.7 copy.26
  (1 shorter events, 0.0 us)

commit v2 on v1

--- a/solution.py
+++ b/solution.py
@@ -3,6 +3,7 @@
 
 import jax
 import jax.numpy as jnp
+import numpy as np
 from jax import lax
 from jax.experimental import pallas as pl
 from jax.experimental.pallas import tpu as pltpu
@@ -50,10 +51,12 @@
 
 
 def kernel(
-    x_ref, cot_ref, pos_ref, cos_ref, sin_ref, gain_ref, wq_hbm, wk_hbm, wv_hbm, wo_hbm,
+    x_ref, cot_ref, pos_ref, gain_ref, freq_ref, wq_hbm, wk_hbm, wv_hbm, wo_hbm,
     hidden_ref, gin_ref, dwq_ref, dwk_ref, dwv_ref, dwo_ref,
     w, wo, wot, xt, xa, part, bg, bgt, att_all, att, qt, ga, kv, s_scr, p_scr, wt_scr, g_all,
     acc, r_core, r_x, r_x2, r_z, s_buf, branch, stat, halo_out, halo_in, halo_prev, halo_z, dw_out, dw_in,
+    trig, gain_t, scaled_t,
+    ds_scr,
     load_sem, ag_s, ag_r, rs_s, rs_r, st_s, st_r, kv_s, kv_r, xa_s, xa_r, at_s, at_r, pm_s, pm_r,
     ha_s, ha_r, g_s, g_r, dw_s, dw_r,
 ):
@@ -78,21 +81,22 @@
         return pl.ds(pl.multiple_of(index * size, 16), size)
 
     pending = []
-
-    def push(src, dst, ssem, rsem, device):
+    tail = []
+
+    def send(src, dst, sems, k, device):
         copy = pltpu.make_async_remote_copy(
-            src_ref=src, dst_ref=dst, send_sem=ssem, recv_sem=rsem, device_id=device, device_id_type=MESH
+            src_ref=src, dst_ref=dst, send_sem=sems[0].at[k], recv_sem=sems[1].at[k],
+            device_id=device, device_id_type=MESH,
         )
         copy.start()
-        return copy
-
-    def send(*args):
-        pending.append(push(*args))
-
-    def landed(dst, ssem, rsem):
+        pending.append(copy)
+
+    def landed(dst, sems, k):
         pltpu.make_async_remote_copy(
-            src_ref=dst, dst_ref=dst, send_sem=ssem, recv_sem=rsem, device_id=at_y(1), device_id_type=MESH
+            src_ref=dst, dst_ref=dst, send_sem=sems[0].at[k], recv_sem=sems[1].at[k],
+            device_id=at_y(1), device_id_type=MESH,
         ).wait_recv()
+
 
     loads = []
     for i, (src, dst) in enumerate(
@@ -125,18 +129,18 @@
     def _():
         pl.semaphore_wait(barrier, 21)
 
-    def gather(buf, ss, rs):
+    def gather(buf, sems):
         def key(o):
             return o[0] * 8 + o[1] * 2 + o[2]
 
         def forward(o, e):
             rel = ((o[0] + e[0]) % 2, (o[1] - e[1]) % 4, (o[2] + e[2]) % 2)
             block = buf.at[rows(head_of(o)), :]
-            send(block, block, ss.at[key(rel)], rs.at[key(rel)], at_head(e))
+            send(block, block, sems, key(rel), at_head(e))
 
         def wait(o):
             block = buf.at[rows(head_of(o)), :]
-            landed(block, ss.at[key(o)], rs.at[key(o)])
+            landed(block, sems, key(o))
 
         def begin():
             for e in ((1, 0, 0), (0, 1, 0), (0, 3, 0), (0, 2, 0), (0, 0, 1)):
@@ -152,24 +156,35 @@
             ((1, 2), ((0, 0, 1),)),
         )
 
+        def relay(chip, targets):
+            wait((chip[0], chip[1], 0))
+            for e in targets:
+                forward((chip[0], chip[1], 0), e)
+
+        def take(chip, consume):
+            wait((chip[0], chip[1], 1))
+            consume(head_of((chip[0], chip[1], 0)) // 2)
+
         def finish(consume):
-            def take(chip):
-                wait((chip[0], chip[1], 1))
-                consume(head_of((chip[0], chip[1], 0)) // 2)
-
             last = (0, 0)
             for chip, targets in events:
-                wait((chip[0], chip[1], 0))
-                for e in targets:
-                    forward((chip[0], chip[1], 0), e)
-                take(last)
+                relay(chip, targets)
+                take(last, consume)
                 last = chip
-            take(last)
-
-        return begin, finish
+            take(last, consume)
+
+        def relays(first, end):
+            for chip, targets in events[first:end]:
+                relay(chip, targets)
+
+        def takes(consume):
+            for chip in ((0, 0),) + tuple(chip for chip, _ in events):
+                take(chip, consume)
+
+        return begin, finish, relays, takes
 
     def scatter(produce, k):
-        ss, rs = rs_s.at[k], rs_r.at[k]
+        sems = (rs_s.at[k], rs_r.at[k], (1, k))
         rc, rx, rx2, rz, sb, pt = r_core.at[k], r_x.at[k], r_x2.at[k], r_z.at[k], s_buf.at[k], part.at[k]
         order = ((1, 2), (1, 1), (1, 3), (0, 1), (0, 3), (0, 2), (1, 0), (0, 0))
 
@@ -177,47 +192,54 @@
             chip = head_of((order[i][0], order[i][1], 0)) // 2
             pt[rows(chip, PAIR), :] = produce(chip).astype(BF16)
             block = pt.at[rows(chip * 2 + 1 - q), :]
-            send(block, rc.at[i], ss.at[i], rs.at[i], at_head((0, 0, 1)))
+            send(block, rc.at[i], sems, i, at_head((0, 0, 1)))
 
         def settle(i):
             dz, dx = order[i]
-            landed(rc.at[i], ss.at[i], rs.at[i])
+            landed(rc.at[i], sems, i)
             total = pt[rows(head_of((dz, dx, 0))), :].astype(F32) + rc[i].astype(F32)
             if (dz, dx) == (1, 2):
                 sb[i] = total.astype(BF16)
-                send(sb.at[i], rz.at[0], ss.at[8], rs.at[8], at_head((1, 0, 0)))
+                send(sb.at[i], rz.at[0], sems, 8, at_head((1, 0, 0)))
             elif dx in (1, 3):
                 j = (dx // 2) * 2 + dz
                 sb[i] = total.astype(BF16)
-                send(sb.at[i], rx.at[j], ss.at[9 + j], rs.at[9 + j], at_head((0, dx, 0)))
+                send(sb.at[i], rx.at[j], sems, 9 + j, at_head((0, dx, 0)))
             elif (dz, dx) == (0, 2):
-                landed(rz.at[0], ss.at[8], rs.at[8])
+                landed(rz.at[0], sems, 8)
                 sb[i] = (total + rz[0].astype(F32)).astype(BF16)
-                send(sb.at[i], rx2, ss.at[13], rs.at[13], at_head((0, 2, 0)))
+                send(sb.at[i], rx2, sems, 13, at_head((0, 2, 0)))
             elif (dz, dx) == (1, 0):
                 for j in (1, 3):
-                    landed(rx.at[j], ss.at[9 + j], rs.at[9 + j])
+                    landed(rx.at[j], sems, 9 + j)
                     total = total + rx[j].astype(F32)
                 sb[i] = total.astype(BF16)
-                send(sb.at[i], rz.at[1], ss.at[14], rs.at[14], at_head((1, 0, 0)))
+                send(sb.at[i], rz.at[1], sems, 14, at_head((1, 0, 0)))
             else:
                 for j in (0, 2):
-                    landed(rx.at[j], ss.at[9 + j], rs.at[9 + j])
+                    landed(rx.at[j], sems, 9 + j)
                     total = total + rx[j].astype(F32)
-                landed(rx2, ss.at[13], rs.at[13])
+                landed(rx2, sems, 13)
                 total = total + rx2[...].astype(F32)
-                landed(rz.at[1], ss.at[14], rs.at[14])
+                landed(rz.at[1], sems, 14)
                 total = total + rz[1].astype(F32)
                 return total
             return None
 
-        for i in range(8):
-            make(i)
-            if i > 0:
-                settle(i - 1)
-        return settle(7)
-
-    ag_begin, ag_finish = gather(xt, ag_s.at[0], ag_r.at[0])
+        def first():
+            for i in range(8):
+                make(i)
+                if 0 < i < 6:
+                    settle(i - 1)
+
+        def second():
+            settle(5)
+            settle(6)
+            return settle(7)
+
+        return first, second
+
+    ag_begin, ag_finish, _, _ = gather(xt, (ag_s.at[0], ag_r.at[0], (0, 0)))
     ag_begin()
     acc[...] = jnp.zeros_like(acc)
     loads[3].wait()
@@ -228,6 +250,11 @@
         return carry
 
     lax.fori_loop(0, D // 128, turn, 0)
+    angles = freq_ref[...] * pos_ref[...].astype(F32)
+    trig[0] = jnp.cos(angles)
+    trig[1] = jnp.sin(angles)
+    gain_t[...] = dot_tn(gain_ref[...].reshape(1, BLK), jnp.ones((1, T), BF16))
+    scaled_t[...] = cot_ref[...].astype(F32) * gain_t[...]
     for cp in loads[:3]:
         cp.wait()
 
@@ -235,7 +262,7 @@
         acc[...] += dot_tn(w[rows(chip, PAIR), :], xt[rows(chip, PAIR), :])
 
     ag_finish(project)
-    cos, sin = cos_ref[...], sin_ref[...]
+    cos, sin = trig[0], trig[1]
     qt[:, 0:T] = rot(acc[0:128, :], cos, sin).astype(BF16)
     qt[:, T : 2 * T] = rot(acc[128:256, :], cos, sin).astype(BF16)
     kv[4, 0:128, :] = rot(acc[256:384, :], cos, sin).astype(BF16)
@@ -276,6 +303,16 @@
         @pl.when(y + r >= 4)
         def _():
             kv_out(0, r).start()
+
+    def kv_sent():
+        for r in (1, 2, 3):
+            kv_out(0, r).wait_send()
+
+        @pl.when(zh < 3)
+        def _():
+            kv_up().wait_send()
+
+    tail.append(kv_sent)
 
     lane = lax.broadcasted_iota(jnp.int32, (1, T), 1)
     limit = jnp.minimum(jnp.minimum(pos_ref[...], WINDOW - 1), lane + c * T)
@@ -304,6 +341,13 @@
         highest = lax.fori_loop(0, T // STEP, mask, highest)
     highest = jnp.max(highest, axis=0, keepdims=True)
 
+    for r in (1, 2, 3):
+        for j in range(2):
+            dz = q * 2 + j
+            send(
+                xt.at[rows(dz * 4 + (y + r) % 4), :], xa.at[r - 1, dz], (xa_s, xa_r, 4), (r - 1) * 2 + j, at_y(r)
+            )
+
     def expo(i, total):
         at = pl.multiple_of(i * STEP, STEP)
         slot, at = i // (T // STEP), pl.multiple_of((i % (T // STEP)) * STEP, STEP)
@@ -316,9 +360,7 @@
 
     def norm(i, carry):
         slot, at = i // (T // STEP), pl.multiple_of((i % (T // STEP)) * STEP, STEP)
-        p = p_scr[slot, pl.ds(at, STEP), :] * recip
-        p_scr[slot, pl.ds(at, STEP), :] = p
-        wt_scr[slot, pl.ds(at, STEP), :] = p.astype(BF16)
+        wt_scr[slot, pl.ds(at, STEP), :] = (p_scr[slot, pl.ds(at, STEP), :] * recip).astype(BF16)
         return carry
 
     lax.fori_loop(0, 5 * T // STEP, norm, 0)
@@ -330,33 +372,25 @@
     att[128:256, :] = out[:, T : 2 * T]
     att_all[c] = att[...]
 
-    for r in (1, 2, 3):
-        send(att, att_all.at[c], at_s.at[r], at_r.at[r], at_z(r))
-
     def project_out(chip):
         return dot_nn(wot[rows(chip, PAIR), :], att[...])
 
-    branch[...] = scatter(project_out, 0)
-    gain = gain_ref[...]
-    scaled = cot_ref[...].astype(F32) * gain
+    out_first, out_second = scatter(project_out, 0)
+    out_first()
+    for r in (1, 2, 3):
+        send(att, att_all.at[c], (at_s, at_r, 2), r, at_z(r))
+    branch[...] = out_second()
+    gain = gain_t[...]
+    scaled = scaled_t[...]
     stat[h] = jnp.zeros((8, T), F32)
     stat[h, 0:1, :] = jnp.sum(branch[...] * branch[...], axis=0, keepdims=True)
     stat[h, 1:2, :] = jnp.sum(scaled * branch[...], axis=0, keepdims=True)
     for i, o in enumerate(others):
-        send(stat.at[h], stat.at[h], st_s.at[i], st_r.at[i], at_head(o))
-
-    for r in (1, 2, 3):
-        source = ((zh + 4 - r) % 4) * 4 + y
-        landed(att_all.at[source], at_s.at[r], at_r.at[r])
-    for r in (1, 2, 3):
-        for dz in range(4):
-            block = att_all.at[((zh + dz) % 4) * 4 + y]
-            i = 4 + (r - 1) * 4 + dz
-            send(block, block, at_s.at[i], at_r.at[i], at_y(r))
+        send(stat.at[h], stat.at[h], (st_s, st_r, 3), i, at_head(o))
 
     for i, o in enumerate(others):
         back = head_of((o[0], (4 - o[1]) % 4, o[2]))
-        landed(stat.at[back], st_s.at[i], st_r.at[i])
+        landed(stat.at[back], (st_s, st_r, 3), i)
     sums = stat[0]
     for i in range(1, 16):
         sums = sums + stat[i]
@@ -364,8 +398,16 @@
     slopes = inverse * sums[1:2] / D
     normed = branch[...] * inverse
     bg[rows(h), :] = (inverse * (scaled - normed * slopes)).astype(BF16)
-    bg_begin, bg_finish = gather(bg, ag_s.at[1], ag_r.at[1])
+    bg_begin, bg_finish, _, _ = gather(bg, (ag_s.at[1], ag_r.at[1], (0, 1)))
     bg_begin()
+    for r in (1, 2, 3):
+        source = ((zh + 4 - r) % 4) * 4 + y
+        landed(att_all.at[source], (at_s, at_r, 2), r)
+    for r in (1, 2, 3):
+        for dz in range(4):
+            block = att_all.at[((zh + dz) % 4) * 4 + y]
+            i = 4 + (r - 1) * 4 + dz
+            send(block, block, (at_s, at_r, 2), i, at_y(r))
     hidden_ref[...] = (x_ref[...].astype(F32) + normed * gain).astype(BF16)
 
     def mirror():
@@ -384,16 +426,16 @@
     def _():
         mirror().start()
 
+    def mirror_sent():
+        @pl.when(c != h)
+        def _():
+            mirror().wait_send()
+
+    tail.append(mirror_sent)
+
     @pl.when(c == h)
     def _():
         bgt[rows(h), :] = bg[rows(h), :]
-
-    for r in (1, 2, 3):
-        for dz in range(4):
-            i = (r - 1) * 4 + dz
-            send(
-                xt.at[rows(dz * 4 + (y + r) % 4), :], xa.at[r - 1, dz], xa_s.at[i], xa_r.at[i], at_y(r)
-            )
 
     acc[0:256, :] = jnp.zeros((256, T), F32)
 
@@ -408,8 +450,13 @@
     def _():
         mirrored().wait_recv()
 
-    bgt_begin, bgt_finish = gather(bgt, ag_s.at[2], ag_r.at[2])
+    bgt_begin, _, bgt_relays, bgt_takes = gather(bgt, (ag_s.at[2], ag_r.at[2], (0, 2)))
     bgt_begin()
+    for r in (1, 2, 3):
+        for j in range(2):
+            block = xa.at[r - 1, q * 2 + j]
+            landed(block, (xa_s, xa_r, 4), (r - 1) * 2 + j)
+            send(block, block, (xa_s, xa_r, 4), 6 + (r - 1) * 2 + j, at_head((0, 0, 1)))
 
     inner = jnp.zeros((8, 2 * T), F32)
     for slot in range(5):
@@ -419,55 +466,43 @@
         slot, at = i // (T // STEP), pl.multiple_of((i % (T // STEP)) * STEP, STEP)
         return total + fold(p_scr[slot, pl.ds(at, STEP), :] * s_scr[slot, pl.ds(at, STEP), :])
 
-    inner = jnp.sum(lax.fori_loop(0, 5 * T // STEP, weigh, inner), axis=0, keepdims=True)
-
-    ds = acc_ds = None
-    dq = None
-    own_kv = None
+    inner = jnp.sum(lax.fori_loop(0, 5 * T // STEP, weigh, inner), axis=0, keepdims=True) * recip
+
+    def grad(i, carry):
+        slot, at = i // (T // STEP), pl.multiple_of((i % (T // STEP)) * STEP, STEP)
+        p = p_scr[slot, pl.ds(at, STEP), :] * recip
+        ds_scr[slot, pl.ds(at, STEP), :] = (p * (s_scr[slot, pl.ds(at, STEP), :] - inner)).astype(BF16)
+        return carry
+
+    lax.fori_loop(0, 5 * T // STEP, grad, 0)
+    dq = dot_nn(kv[0, 0:128, :], ds_scr[0])
+    for slot in range(1, 5):
+        dq = dq + dot_nn(kv[slot, 0:128, :], ds_scr[slot])
+    dq = dq * SCALE
+    g_all[0, 0:128, :] = rot(dq[:, 0:T], cos, -sin).astype(BF16)
+    g_all[0, 128:256, :] = rot(dq[:, T : 2 * T], cos, -sin).astype(BF16)
+    for r in (1, 2, 3):
+        send(
+            g_all.at[0, 0:256, :], g_all.at[r, 0:256, :], (g_s, g_r, 6), r - 1, at_y(r)
+        )
+
     for slot in (1, 2, 3, 0, 4):
-
-        def grad(i, carry, slot=slot):
-            at = pl.multiple_of(i * STEP, STEP)
-            p = p_scr[slot, pl.ds(at, STEP), :]
-            d = p * (s_scr[slot, pl.ds(at, STEP), :] - inner)
-            part[1, pl.ds(pl.multiple_of(slot * 512 + at, STEP), STEP), :] = d[:, 0:T].astype(BF16)
-            part[1, pl.ds(pl.multiple_of(slot * 512 + 256 + at, STEP), STEP), :] = d[:, T : 2 * T].astype(BF16)
-            return carry
-
-        lax.fori_loop(0, T // STEP, grad, 0)
-        d0 = part[1, slot * 512 : slot * 512 + 256, :]
-        d1 = part[1, slot * 512 + 256 : slot * 512 + 512, :]
-        dk = (dot_nt(qt[:, 0:T], d0) + dot_nt(qt[:, T : 2 * T], d1)) * SCALE
+        dk = dot_nt(qt[...], ds_scr[slot]) * SCALE
         dv = dot_nt(ga[...], wt_scr[slot])
         if slot in (1, 2, 3):
             halo_out[slot - 1, 0:128, :] = dk.astype(BF16)
             halo_out[slot - 1, 128:256, :] = dv.astype(BF16)
             send(
-                halo_out.at[slot - 1], halo_in.at[slot - 1], ha_s.at[slot], ha_r.at[slot], at_y(slot)
+                halo_out.at[slot - 1], halo_in.at[slot - 1], (ha_s, ha_r, 5), slot, at_y(slot)
             )
         else:
             i = 0 if slot == 0 else 1
             halo_prev[i, 0:128, :] = dk
             halo_prev[i, 128:256, :] = dv
-        k_slot = kv[slot, 0:128, :]
-        part0, part1 = dot_nn(k_slot, d0), dot_nn(k_slot, d1)
-        if dq is None:
-            acc[0:128, :] = part0
-            acc[128:256, :] = part1
-            dq = True
-        else:
-            acc[0:128, :] += part0
-            acc[128:256, :] += part1
-
-    g_all[0, 0:128, :] = rot(acc[0:128, :] * SCALE, cos, -sin).astype(BF16)
-    g_all[0, 128:256, :] = rot(acc[128:256, :] * SCALE, cos, -sin).astype(BF16)
-    for r in (1, 2, 3):
-        send(
-            g_all.at[0, 0:256, :], g_all.at[r, 0:256, :], g_s.at[r - 1], g_r.at[r - 1], at_y(r)
-        )
-
-    for r in (1, 2, 3):
-        landed(halo_in.at[r - 1], ha_s.at[r], ha_r.at[r])
+    bgt_relays(0, 4)
+
+    for r in (1, 2, 3):
+        landed(halo_in.at[r - 1], (ha_s, ha_r, 5), r)
         value = halo_in[r - 1].astype(F32)
         back = (y >= r).astype(F32)
         halo_prev[0] += value * back
@@ -484,28 +519,22 @@
     def _():
         down().start()
 
-    @pl.when(zh < 3)
-    def _():
-        down().wait_recv()
-        halo_prev[1] += halo_z[1].astype(F32)
-
-    g_all[0, 256:384, :] = rot(halo_prev[1, 0:128, :], cos, -sin).astype(BF16)
-    g_all[0, 384:512, :] = halo_prev[1, 128:256, :].astype(BF16)
-    for r in (1, 2, 3):
-        send(
-            g_all.at[0, 256:512, :], g_all.at[r, 256:512, :], g_s.at[r + 2], g_r.at[r + 2], at_y(r)
-        )
-
-    for r in (1, 2, 3):
-        for dz in range(4):
-            i = (r - 1) * 4 + dz
-            landed(xa.at[r - 1, dz], xa_s.at[i], xa_r.at[i])
+    def down_sent():
+        @pl.when(zh > 0)
+        def _():
+            down().wait_send()
+
+    tail.append(down_sent)
+
+    for r in (1, 2, 3):
+        for j in range(2):
+            landed(xa.at[r - 1, (1 - q) * 2 + j], (xa_s, xa_r, 4), 6 + (r - 1) * 2 + j)
 
     def weight_grads(k):
         lo = k * 256
         for r in (1, 2, 3):
             i = r - 1 + 3 * k
-            landed(g_all.at[r, lo : lo + 256, :], g_s.at[i], g_r.at[i])
+            landed(g_all.at[r, lo : lo + 256, :], (g_s, g_r, 6), i)
         result = None
         for dz in (1, 2, 3, 0):
             z = (zh + dz) % 4
@@ -517,63 +546,70 @@
             else:
                 i = k * 3 + dz - 1
                 dw_out[i] = total.astype(BF16)
-                send(dw_out.at[i], dw_in.at[i], dw_s.at[i], dw_r.at[i], at_z(dz))
+                send(dw_out.at[i], dw_in.at[i], (dw_s, dw_r, 7), i, at_z(dz))
         return result
 
     dwq_ref[...] = weight_grads(0)
+    bgt_relays(4, 7)
+
+    @pl.when(zh < 3)
+    def _():
+        down().wait_recv()
+        halo_prev[1] += halo_z[1].astype(F32)
+
+    g_all[0, 256:384, :] = rot(halo_prev[1, 0:128, :], cos, -sin).astype(BF16)
+    g_all[0, 384:512, :] = halo_prev[1, 128:256, :].astype(BF16)
+    for r in (1, 2, 3):
+        send(
+            g_all.at[0, 256:512, :], g_all.at[r, 256:512, :], (g_s, g_r, 6), r + 2, at_y(r)
+        )
+
 
     def input_terms(chip):
         return dot_nn(w[rows(chip, PAIR), :], g_all[0])
 
+    in_first, in_second = scatter(input_terms, 1)
+    in_first()
     dkv = weight_grads(1)
     dwk_ref[...] = dkv[:, 0:128]
     dwv_ref[...] = dkv[:, 128:256]
-    gin_ref[...] = (cot_ref[...].astype(F32) + scatter(input_terms, 1)).astype(BF16)
+    gin_ref[...] = (cot_ref[...].astype(F32) + in_second()).astype(BF16)
 
     for r in (1, 2, 3):
         for dz in range(4):
             block = att_all.at[((zh + dz) % 4) * 4 + (y + 4 - r) % 4]
             i = 4 + (r - 1) * 4 + dz
-            landed(block, at_s.at[i], at_r.at[i])
+            landed(block, (at_s, at_r, 2), i)
     dwo_ref[...] = jnp.zeros_like(dwo_ref)
 
     def out_grad(chip):
         for j in range(2):
             dwo_ref[...] += dot_nt(bgt[rows(chip * 2 + j), :], att_all[chip * 2 + j])
 
-    bgt_finish(out_grad)
+    bgt_takes(out_grad)
 
     for dz in (1, 2, 3):
-        landed(dw_in.at[dz - 1], dw_s.at[dz - 1], dw_r.at[dz - 1])
+        landed(dw_in.at[dz - 1], (dw_s, dw_r, 7), dz - 1)
         dwq_ref[...] += dw_in[dz - 1].astype(F32)
     for dz in (1, 2, 3):
-        landed(dw_in.at[dz + 2], dw_s.at[dz + 2], dw_r.at[dz + 2])
+        landed(dw_in.at[dz + 2], (dw_s, dw_r, 7), dz + 2)
         value = dw_in[dz + 2].astype(F32)
         dwk_ref[...] += value[:, 0:128]
         dwv_ref[...] += value[:, 128:256]
 
     for copy in pending:
         copy.wait_send()
-    for r in (1, 2, 3):
-        kv_out(0, r).wait_send()
-
-    @pl.when(zh < 3)
-    def _():
-        kv_up().wait_send()
-
-    @pl.when(zh > 0)
-    def _():
-        down().wait_send()
-
-    @pl.when(c != h)
-    def _():
-        mirror().wait_send()
+    for wait in tail:
+        wait()
+
+
+def settle(*refs):
+    for i in range(6):
+        refs[6 + i][...] = refs[i][...]
 
 
 def local(inputs, positions, w_query, w_key, w_value, w_out, post_gain, cotangent):
-    half = HD // 2
-    frequency = jnp.exp(jnp.arange(half, dtype=F32) * (-2.0 * math.log(ROPE_BASE) / HD))
-    angles = frequency[:, None] * positions.astype(F32)[None, :]
+    frequency = np.exp(np.arange(HD // 2, dtype=np.float32) * np.float32(-2.0 * math.log(ROPE_BASE) / HD))[:, None]
     vmem = pl.BlockSpec(memory_space=pltpu.VMEM)
     hbm = pl.BlockSpec(memory_space=pl.ANY)
     dma = pltpu.SemaphoreType.DMA
@@ -609,6 +645,10 @@
         pltpu.VMEM((2, 256, T), BF16),
         pltpu.VMEM((6, BLK, T), BF16),
         pltpu.VMEM((6, BLK, T), BF16),
+        pltpu.VMEM((2, HD // 2, T), F32),
+        pltpu.VMEM((BLK, T), F32),
+        pltpu.VMEM((BLK, T), F32),
+        pltpu.VMEM((5, T, 2 * T), BF16),
         dma((4,)),
         dma((3, 16)), dma((3, 16)),
         dma((2, 15)), dma((2, 15)),
@@ -629,10 +669,10 @@
         jax.ShapeDtypeStruct((BLK, 128), F32),
         jax.ShapeDtypeStruct((BLK, 256), F32),
     )
-    hidden, gin, dwq, dwk, dwv, dwo = pl.pallas_call(
+    results = pl.pallas_call(
         kernel,
         out_shape=shapes,
-        in_specs=[vmem] * 6 + [hbm] * 4,
+        in_specs=[vmem] * 5 + [hbm] * 4,
         out_specs=(vmem,) * 6,
         scratch_shapes=scratch,
         compiler_params=pltpu.CompilerParams(
@@ -640,9 +680,16 @@
         ),
         name="layer",
     )(
-        inputs.T, cotangent.T, positions[None, :], jnp.cos(angles), jnp.sin(angles),
-        post_gain.astype(F32)[:, None], w_query, w_key, w_value, w_out,
+        inputs.T, cotangent.T, positions[None, :], post_gain, frequency,
+        w_query, w_key, w_value, w_out,
     )
+    hidden, gin, dwq, dwk, dwv, dwo = pl.pallas_call(
+        settle,
+        out_shape=shapes,
+        in_specs=[vmem] * 6,
+        out_specs=(vmem,) * 6,
+        name="results",
+    )(*results)
     return hidden.T, gin.T, dwq, dwk, dwv, dwo.T
 
 

time: 211 us -> 167 us (0.79)
  Pallas kernels: 194 us -> 165 us
  local copies, waits for them, and re-layouts: 11.3 us -> 0 us
    pallas_call x1 -> x2, Pallas kernels: 194 us -> 165 us  [the longest x1 162 us: local(): pl.pallas_call(kernel, out_shape=shapes, in_specs=[vmem] * 5 + [hbm] * 4,...]
    unnamed x6 -> x0, local copies, waits for them, and re-layouts: 9.85 us -> none
where the time goes in v2:
time: 167 us; the launch traced here: 165 us
  Pallas kernels  165 us (99%)
    pallas_call x1, Pallas kernels, local(): pl.pallas_call(kernel, out_shape=shapes, in_specs=[vmem] * 5 + [hbm] * 4,...  162 us

profile of v2, /device:TPU:1, one launch (start us, length us, event | category | flops | bytes accessed | tf_op | source)
XLA Modules:
  0.0 165.4 jit_solution(13417917957157713849)
XLA Ops:
  0.6 162.3 %layer.1 = (bf16[336,256]{1,0:T(8,128)(2,1)}, bf16[336,256]{1,0:T(8,128)(2,1)}, f32[336,256]{1,0:T(8,128)}, f32[336,128]{1,0:T(8,128)}, f32[336,128]{1,0:T(8,128)}, /*index=5*/f32[336,256]{1,0:T(8,128)}) custom-call(bf16[336,256]{1,0:T(8,128)(2,1)} %bitcast.6, bf16[336,256]{1,0:T(8,128)(2,1)} %bitcast.7, s32[1,256]{1,0:T(1,128)} %bitcast.8, ...), custom_call_target="tpu_custom_call" | custom-call | tf_op jit(solution)/shard_map/layer/pallas_call | solution.py:672
  162.9 2.5 %results.1 = (bf16[336,256]{1,0:T(8,128)(2,1)}, bf16[336,256]{1,0:T(8,128)(2,1)}, f32[336,256]{1,0:T(8,128)}, f32[336,128]{1,0:T(8,128)}, f32[336,128]{1,0:T(8,128)}, /*index=5*/f32[336,256]{1,0:T(8,128)}) custom-call(bf16[336,256]{1,0:T(8,128)(2,1)} %get-tuple-element.18.refs_0_, bf16[336,256]{1,0:T(8,128)(2,1)} %get-tuple-element.19.refs_1_, ...), custom_call_target="tpu_custom_call" | custom-call | tf_op jit(solution)/shard_map/results/pallas_call | solution.py:686

commit v3 on v2

--- a/solution.py
+++ b/solution.py
@@ -18,6 +18,7 @@
 T = 256
 BLK = 336
 PAIR = 672
+HALF = 176
 MESH = pl.DeviceIdType.MESH
 F32 = jnp.float32
 BF16 = jnp.bfloat16
@@ -268,49 +269,62 @@
     kv[4, 0:128, :] = rot(acc[256:384, :], cos, sin).astype(BF16)
     kv[4, 128:256, :] = acc[384:512, :].astype(BF16)
 
-    def kv_out(slot, r):
+    def piece(slot, p):
+        return kv.at[slot, p * 128 : (p + 1) * 128, :]
+
+    def kv_out(slot, r, p):
         return pltpu.make_async_remote_copy(
-            src_ref=kv.at[slot], dst_ref=kv.at[4 - r], send_sem=kv_s.at[r], recv_sem=kv_r.at[r],
+            src_ref=piece(slot, p), dst_ref=piece(4 - r, p), send_sem=kv_s.at[p, r], recv_sem=kv_r.at[p, r],
             device_id=at_y(r), device_id_type=MESH,
         )
 
-    def kv_up():
+    def kv_up(p):
         return pltpu.make_async_remote_copy(
-            src_ref=kv.at[4], dst_ref=kv.at[0], send_sem=kv_s.at[0], recv_sem=kv_r.at[0],
+            src_ref=piece(4, p), dst_ref=piece(0, p), send_sem=kv_s.at[p, 0], recv_sem=kv_r.at[p, 0],
             device_id=at_z(1), device_id_type=MESH,
         )
 
     @pl.when(zh < 3)
     def _():
-        kv_up().start()
-
-    for r in (1, 2, 3):
-
-        @pl.when(y + r < 4)
+        kv_up(0).start()
+
+    for p in (0, 1):
+        for r in (1, 2, 3):
+
+            @pl.when(y + r < 4)
+            def _():
+                kv_out(4, r, p).start()
+
+    @pl.when(zh == 0)
+    def _():
+        kv[0] = jnp.zeros((256, T), BF16)
+
+    @pl.when(zh < 3)
+    def _():
+        kv_up(0).wait_send()
+        kv_up(1).start()
+
+    def relay_kv(p):
+        @pl.when(zh > 0)
         def _():
-            kv_out(4, r).start()
-
-    @pl.when(zh == 0)
-    def _():
-        kv[0] = jnp.zeros((256, T), BF16)
-
-    @pl.when(zh > 0)
-    def _():
-        kv_up().wait_recv()
-
-    for r in (1, 2, 3):
-
-        @pl.when(y + r >= 4)
-        def _():
-            kv_out(0, r).start()
+            kv_up(p).wait_recv()
+
+        for r in (1, 2, 3):
+
+            @pl.when(y + r >= 4)
+            def _():
+                kv_out(0, r, p).start()
+
+    relay_kv(0)
 
     def kv_sent():
-        for r in (1, 2, 3):
-            kv_out(0, r).wait_send()
+        for p in (0, 1):
+            for r in (1, 2, 3):
+                kv_out(0, r, p).wait_send()
 
         @pl.when(zh < 3)
         def _():
-            kv_up().wait_send()
+            kv_up(1).wait_send()
 
     tail.append(kv_sent)
 
@@ -324,8 +338,10 @@
 
     highest = jnp.full((8, 2 * T), -jnp.inf, F32)
     for slot in (4, 0, 3, 1, 2):
+        if slot == 3:
+            relay_kv(1)
         if slot in (1, 2, 3):
-            kv_out(0, 4 - slot).wait_recv()
+            kv_out(0, 4 - slot, 0).wait_recv()
         s_scr[slot] = dot_tn(kv[slot, 0:128, :], qt[...])
 
         def mask(i, top, slot=slot):
@@ -340,6 +356,9 @@
 
         highest = lax.fori_loop(0, T // STEP, mask, highest)
     highest = jnp.max(highest, axis=0, keepdims=True)
+
+    for r in (1, 2, 3):
+        kv_out(0, r, 1).wait_recv()
 
     for r in (1, 2, 3):
         for j in range(2):
@@ -446,12 +465,6 @@
     ga[:, 0:T] = acc[0:128, :].astype(BF16)
     ga[:, T : 2 * T] = acc[128:256, :].astype(BF16)
 
-    @pl.when(c != h)
-    def _():
-        mirrored().wait_recv()
-
-    bgt_begin, _, bgt_relays, bgt_takes = gather(bgt, (ag_s.at[2], ag_r.at[2], (0, 2)))
-    bgt_begin()
     for r in (1, 2, 3):
         for j in range(2):
             block = xa.at[r - 1, q * 2 + j]
@@ -499,14 +512,70 @@
             i = 0 if slot == 0 else 1
             halo_prev[i, 0:128, :] = dk
             halo_prev[i, 128:256, :] = dv
-    bgt_relays(0, 4)
+    @pl.when(c != h)
+    def _():
+        mirrored().wait_recv()
+
+    bgt_begin, _, bgt_relays, bgt_takes = gather(bgt, (ag_s.at[2], ag_r.at[2], (0, 2)))
+    bgt_begin()
+
+    low, high = slice(0, HALF), slice(HALF, BLK)
+
+    def weight_grads(k):
+        sems = (dw_s.at[k], dw_r.at[k], (7, k))
+        lo = k * 256
+        up, far, back = dw_out.at[k * 3], dw_out.at[k * 3 + 1], dw_out.at[k * 3 + 2]
+        mid, in_up, in_back = dw_in.at[k * 3], dw_in.at[k * 3 + 1], dw_in.at[k * 3 + 2]
+
+        def product(dz):
+            z = (zh + dz) % 4
+            total = dot_nt(xt[rows(z * 4 + y), :], g_all[0, lo : lo + 256, :])
+            for r in (1, 2, 3):
+                total = total + dot_nt(xa[r - 1, z], g_all[r, lo : lo + 256, :])
+            return total
+
+        def begin():
+            for r in (1, 2, 3):
+                landed(g_all.at[r, lo : lo + 256, :], (g_s, g_r, 6), r - 1 + 3 * k)
+            far[...] = product(2).astype(BF16)
+            send(far.at[low, :], mid.at[low, :], sems, 0, at_z(1))
+            send(far.at[high, :], mid.at[high, :], sems, 1, at_z(3))
+            up[...] = product(1).astype(BF16)
+            send(up.at[high, :], in_up.at[high, :], sems, 2, at_z(1))
+            back[...] = product(3).astype(BF16)
+            send(back.at[low, :], in_back.at[low, :], sems, 3, at_z(3))
+            return product(0)
+
+        def follow():
+            landed(mid.at[low, :], sems, 0)
+            up[low, :] = (up[low, :].astype(F32) + mid[low, :].astype(F32)).astype(BF16)
+            send(up.at[low, :], in_up.at[low, :], sems, 4, at_z(1))
+            landed(mid.at[high, :], sems, 1)
+            back[high, :] = (back[high, :].astype(F32) + mid[high, :].astype(F32)).astype(BF16)
+            send(back.at[high, :], in_back.at[high, :], sems, 5, at_z(3))
+
+        def received():
+            landed(in_up.at[high, :], sems, 2)
+            landed(in_back.at[low, :], sems, 3)
+            landed(in_up.at[low, :], sems, 4)
+            landed(in_back.at[high, :], sems, 5)
+            return in_up[...].astype(F32) + in_back[...].astype(F32)
+
+        return begin, follow, received
+
+    for r in (1, 2, 3):
+        for j in range(2):
+            landed(xa.at[r - 1, (1 - q) * 2 + j], (xa_s, xa_r, 4), 6 + (r - 1) * 2 + j)
+    wq_begin, wq_follow, wq_received = weight_grads(0)
+    wkv_begin, wkv_follow, wkv_received = weight_grads(1)
+    dwq_ref[...] = wq_begin()
 
     for r in (1, 2, 3):
         landed(halo_in.at[r - 1], (ha_s, ha_r, 5), r)
         value = halo_in[r - 1].astype(F32)
-        back = (y >= r).astype(F32)
-        halo_prev[0] += value * back
-        halo_prev[1] += value * (1.0 - back)
+        earlier = (y >= r).astype(F32)
+        halo_prev[0] += value * earlier
+        halo_prev[1] += value * (1.0 - earlier)
     halo_z[0] = halo_prev[0].astype(BF16)
 
     def down():
@@ -525,32 +594,8 @@
             down().wait_send()
 
     tail.append(down_sent)
-
-    for r in (1, 2, 3):
-        for j in range(2):
-            landed(xa.at[r - 1, (1 - q) * 2 + j], (xa_s, xa_r, 4), 6 + (r - 1) * 2 + j)
-
-    def weight_grads(k):
-        lo = k * 256
-        for r in (1, 2, 3):
-            i = r - 1 + 3 * k
-            landed(g_all.at[r, lo : lo + 256, :], (g_s, g_r, 6), i)
-        result = None
-        for dz in (1, 2, 3, 0):
-            z = (zh + dz) % 4
-            total = dot_nt(xt[rows(z * 4 + y), :], g_all[0, lo : lo + 256, :])
-            for r in (1, 2, 3):
-                total = total + dot_nt(xa[r - 1, z], g_all[r, lo : lo + 256, :])
-            if dz == 0:
-                result = total
-            else:
-                i = k * 3 + dz - 1
-                dw_out[i] = total.astype(BF16)
-                send(dw_out.at[i], dw_in.at[i], (dw_s, dw_r, 7), i, at_z(dz))
-        return result
-
-    dwq_ref[...] = weight_grads(0)
-    bgt_relays(4, 7)
+    bgt_relays(0, 4)
+    wq_follow()
 
     @pl.when(zh < 3)
     def _():
@@ -564,15 +609,16 @@
             g_all.at[0, 256:512, :], g_all.at[r, 256:512, :], (g_s, g_r, 6), r + 2, at_y(r)
         )
 
-
     def input_terms(chip):
         return dot_nn(w[rows(chip, PAIR), :], g_all[0])
 
     in_first, in_second = scatter(input_terms, 1)
     in_first()
-    dkv = weight_grads(1)
+    dkv = wkv_begin()
     dwk_ref[...] = dkv[:, 0:128]
     dwv_ref[...] = dkv[:, 128:256]
+    bgt_relays(4, 7)
+    wkv_follow()
     gin_ref[...] = (cot_ref[...].astype(F32) + in_second()).astype(BF16)
 
     for r in (1, 2, 3):
@@ -588,14 +634,10 @@
 
     bgt_takes(out_grad)
 
-    for dz in (1, 2, 3):
-        landed(dw_in.at[dz - 1], (dw_s, dw_r, 7), dz - 1)
-        dwq_ref[...] += dw_in[dz - 1].astype(F32)
-    for dz in (1, 2, 3):
-        landed(dw_in.at[dz + 2], (dw_s, dw_r, 7), dz + 2)
-        value = dw_in[dz + 2].astype(F32)
-        dwk_ref[...] += value[:, 0:128]
-        dwv_ref[...] += value[:, 128:256]
+    dwq_ref[...] += wq_received()
+    value = wkv_received()
+    dwk_ref[...] += value[:, 0:128]
+    dwv_ref[...] += value[:, 128:256]
 
     for copy in pending:
         copy.wait_send()
@@ -653,13 +695,13 @@
         dma((3, 16)), dma((3, 16)),
         dma((2, 15)), dma((2, 15)),
         dma((15,)), dma((15,)),
-        dma((4,)), dma((4,)),
+        dma((2, 4)), dma((2, 4)),
         dma((12,)), dma((12,)),
         dma((16,)), dma((16,)),
         dma, dma,
         dma((4,)), dma((4,)),
         dma((6,)), dma((6,)),
-        dma((6,)), dma((6,)),
+        dma((2, 6)), dma((2, 6)),
     ]
     shapes = (
         jax.ShapeDtypeStruct((BLK, T), BF16),

time: 167 us -> 165 us (0.988)
  no operation moved by 1% of the time
where the time goes in v3:
time: 165 us; the launch traced here: 164 us
  Pallas kernels  164 us (99%)
    pallas_call x1, Pallas kernels, local(): pl.pallas_call(kernel, out_shape=shapes, in_specs=[vmem] * 5 + [hbm] * 4,...  161 us

profile of v3, /device:TPU:1, one launch (start us, length us, event | category | flops | bytes accessed | tf_op | source)
XLA Modules:
  0.0 164.4 jit_solution(16652938572932698015)
XLA Ops:
  0.6 161.3 %layer.1 = (bf16[336,256]{1,0:T(8,128)(2,1)}, bf16[336,256]{1,0:T(8,128)(2,1)}, f32[336,256]{1,0:T(8,128)}, f32[336,128]{1,0:T(8,128)}, f32[336,128]{1,0:T(8,128)}, /*index=5*/f32[336,256]{1,0:T(8,128)}) custom-call(bf16[336,256]{1,0:T(8,128)(2,1)} %bitcast.6, bf16[336,256]{1,0:T(8,128)(2,1)} %bitcast.7, s32[1,256]{1,0:T(1,128)} %bitcast.8, ...), custom_call_target="tpu_custom_call" | custom-call | tf_op jit(solution)/shard_map/layer/pallas_call | solution.py:714
  162.0 2.5 %results.1 = (bf16[336,256]{1,0:T(8,128)(2,1)}, bf16[336,256]{1,0:T(8,128)(2,1)}, f32[336,256]{1,0:T(8,128)}, f32[336,128]{1,0:T(8,128)}, f32[336,128]{1,0:T(8,128)}, /*index=5*/f32[336,256]{1,0:T(8,128)}) custom-call(bf16[336,256]{1,0:T(8,128)(2,1)} %get-tuple-element.18.refs_0_, bf16[336,256]{1,0:T(8,128)(2,1)} %get-tuple-element.19.refs_1_, ...), custom_call_target="tpu_custom_call" | custom-call | tf_op jit(solution)/shard_map/results/pallas_call | solution.py:728

commit v4 on v3

--- a/solution.py
+++ b/solution.py
@@ -398,6 +398,13 @@
     out_first()
     for r in (1, 2, 3):
         send(att, att_all.at[c], (at_s, at_r, 2), r, at_z(r))
+
+    def along_y(dz):
+        block = att_all.at[((zh + dz) % 4) * 4 + y]
+        for r in (1, 2, 3):
+            send(block, block, (at_s, at_r, 2), 4 + (r - 1) * 4 + dz, at_y(r))
+
+    along_y(0)
     branch[...] = out_second()
     gain = gain_t[...]
     scaled = scaled_t[...]
@@ -419,14 +426,12 @@
     bg[rows(h), :] = (inverse * (scaled - normed * slopes)).astype(BF16)
     bg_begin, bg_finish, _, _ = gather(bg, (ag_s.at[1], ag_r.at[1], (0, 1)))
     bg_begin()
-    for r in (1, 2, 3):
-        source = ((zh + 4 - r) % 4) * 4 + y
-        landed(att_all.at[source], (at_s, at_r, 2), r)
-    for r in (1, 2, 3):
-        for dz in range(4):
-            block = att_all.at[((zh + dz) % 4) * 4 + y]
-            i = 4 + (r - 1) * 4 + dz
-            send(block, block, (at_s, at_r, 2), i, at_y(r))
+    def attended_on(dz):
+        landed(att_all.at[((zh + dz) % 4) * 4 + y], (at_s, at_r, 2), 4 - dz)
+        along_y(dz)
+
+    attended_on(3)
+    attended_on(1)
     hidden_ref[...] = (x_ref[...].astype(F32) + normed * gain).astype(BF16)
 
     def mirror():
@@ -488,17 +493,6 @@
         return carry
 
     lax.fori_loop(0, 5 * T // STEP, grad, 0)
-    dq = dot_nn(kv[0, 0:128, :], ds_scr[0])
-    for slot in range(1, 5):
-        dq = dq + dot_nn(kv[slot, 0:128, :], ds_scr[slot])
-    dq = dq * SCALE
-    g_all[0, 0:128, :] = rot(dq[:, 0:T], cos, -sin).astype(BF16)
-    g_all[0, 128:256, :] = rot(dq[:, T : 2 * T], cos, -sin).astype(BF16)
-    for r in (1, 2, 3):
-        send(
-            g_all.at[0, 0:256, :], g_all.at[r, 0:256, :], (g_s, g_r, 6), r - 1, at_y(r)
-        )
-
     for slot in (1, 2, 3, 0, 4):
         dk = dot_nt(qt[...], ds_scr[slot]) * SCALE
         dv = dot_nt(ga[...], wt_scr[slot])
@@ -519,6 +513,43 @@
     bgt_begin, _, bgt_relays, bgt_takes = gather(bgt, (ag_s.at[2], ag_r.at[2], (0, 2)))
     bgt_begin()
 
+    dq = dot_nn(kv[0, 0:128, :], ds_scr[0])
+    for slot in range(1, 5):
+        dq = dq + dot_nn(kv[slot, 0:128, :], ds_scr[slot])
+    dq = dq * SCALE
+    g_all[0, 0:128, :] = rot(dq[:, 0:T], cos, -sin).astype(BF16)
+    g_all[0, 128:256, :] = rot(dq[:, T : 2 * T], cos, -sin).astype(BF16)
+
+    for r in (1, 2, 3):
+        landed(halo_in.at[r - 1], (ha_s, ha_r, 5), r)
+        value = halo_in[r - 1].astype(F32)
+        earlier = (y >= r).astype(F32)
+        halo_prev[0] += value * earlier
+        halo_prev[1] += value * (1.0 - earlier)
+    halo_z[0] = halo_prev[0].astype(BF16)
+
+    def down():
+        return pltpu.make_async_remote_copy(
+            src_ref=halo_z.at[0], dst_ref=halo_z.at[1], send_sem=ha_s.at[0], recv_sem=ha_r.at[0],
+            device_id=at_z(3), device_id_type=MESH,
+        )
+
+    @pl.when(zh > 0)
+    def _():
+        down().start()
+
+    def down_sent():
+        @pl.when(zh > 0)
+        def _():
+            down().wait_send()
+
+    tail.append(down_sent)
+
+    for r in (1, 2, 3):
+        send(
+            g_all.at[0, 0:256, :], g_all.at[r, 0:256, :], (g_s, g_r, 6), r - 1, at_y(r)
+        )
+
     low, high = slice(0, HALF), slice(HALF, BLK)
 
     def weight_grads(k):
@@ -568,34 +599,7 @@
             landed(xa.at[r - 1, (1 - q) * 2 + j], (xa_s, xa_r, 4), 6 + (r - 1) * 2 + j)
     wq_begin, wq_follow, wq_received = weight_grads(0)
     wkv_begin, wkv_follow, wkv_received = weight_grads(1)
-    dwq_ref[...] = wq_begin()
-
-    for r in (1, 2, 3):
-        landed(halo_in.at[r - 1], (ha_s, ha_r, 5), r)
-        value = halo_in[r - 1].astype(F32)
-        earlier = (y >= r).astype(F32)
-        halo_prev[0] += value * earlier
-        halo_prev[1] += value * (1.0 - earlier)
-    halo_z[0] = halo_prev[0].astype(BF16)
-
-    def down():
-        return pltpu.make_async_remote_copy(
-            src_ref=halo_z.at[0], dst_ref=halo_z.at[1], send_sem=ha_s.at[0], recv_sem=ha_r.at[0],
-            device_id=at_z(3), device_id_type=MESH,
-        )
-
-    @pl.when(zh > 0)
-    def _():
-        down().start()
-
-    def down_sent():
-        @pl.when(zh > 0)
-        def _():
-            down().wait_send()
-
-    tail.append(down_sent)
     bgt_relays(0, 4)
-    wq_follow()
 
     @pl.when(zh < 3)
     def _():
@@ -608,12 +612,16 @@
         send(
             g_all.at[0, 256:512, :], g_all.at[r, 256:512, :], (g_s, g_r, 6), r + 2, at_y(r)
         )
+    attended_on(2)
+
+    dwq_ref[...] = wq_begin()
 
     def input_terms(chip):
         return dot_nn(w[rows(chip, PAIR), :], g_all[0])
 
     in_first, in_second = scatter(input_terms, 1)
     in_first()
+    wq_follow()
     dkv = wkv_begin()
     dwk_ref[...] = dkv[:, 0:128]
     dwv_ref[...] = dkv[:, 128:256]

time: 165 us -> 158 us (0.958)
  Pallas kernels: 164 us -> 157 us
    pallas_call x1, Pallas kernels: 161 us -> 155 us  [local(): pl.pallas_call(kernel, out_shape=shapes, in_specs=[vmem] * 5 + [hbm] * 4,...]
where the time goes in v4:
time: 158 us
  Pallas kernels  157 us (99%)
    pallas_call x1, Pallas kernels, local(): pl.pallas_call(kernel, out_shape=shapes, in_specs=[vmem] * 5 + [hbm] * 4,...  155 us

profile of v4, /device:TPU:1, one launch (start us, length us, event | category | flops | bytes accessed | tf_op | source)
XLA Modules:
  0.0 157.8 jit_solution(16878839866806142280)
XLA Ops:
  0.6 154.7 %layer.1 = (bf16[336,256]{1,0:T(8,128)(2,1)}, bf16[336,256]{1,0:T(8,128)(2,1)}, f32[336,256]{1,0:T(8,128)}, f32[336,128]{1,0:T(8,128)}, f32[336,128]{1,0:T(8,128)}, /*index=5*/f32[336,256]{1,0:T(8,128)}) custom-call(bf16[336,256]{1,0:T(8,128)(2,1)} %bitcast.6, bf16[336,256]{1,0:T(8,128)(2,1)} %bitcast.7, s32[1,256]{1,0:T(1,128)} %bitcast.8, ...), custom_call_target="tpu_custom_call" | custom-call | tf_op jit(solution)/shard_map/layer/pallas_call | solution.py:722
  155.3 2.5 %results.1 = (bf16[336,256]{1,0:T(8,128)(2,1)}, bf16[336,256]{1,0:T(8,128)(2,1)}, f32[336,256]{1,0:T(8,128)}, f32[336,128]{1,0:T(8,128)}, f32[336,128]{1,0:T(8,128)}, /*index=5*/f32[336,256]{1,0:T(8,128)}) custom-call(bf16[336,256]{1,0:T(8,128)(2,1)} %get-tuple-element.18.refs_0_, bf16[336,256]{1,0:T(8,128)(2,1)} %get-tuple-element.19.refs_1_, ...), custom_call_target="tpu_custom_call" | custom-call | tf_op jit(solution)/shard_map/results/pallas_call | solution.py:736

commit v5 on v4

--- a/solution.py
+++ b/solution.py
@@ -167,12 +167,14 @@
             consume(head_of((chip[0], chip[1], 0)) // 2)
 
         def finish(consume):
-            last = (0, 0)
-            for chip, targets in events:
-                relay(chip, targets)
-                take(last, consume)
-                last = chip
-            take(last, consume)
+            chips = [chip for chip, _ in events]
+            relays(0, 1)
+            take((0, 0), consume)
+            relays(1, 4)
+            for i in range(7):
+                if i in (2, 3, 4):
+                    relays(i + 2, i + 3)
+                take(chips[i], consume)
 
         def relays(first, end):
             for chip, targets in events[first:end]:
@@ -621,10 +623,10 @@
 
     in_first, in_second = scatter(input_terms, 1)
     in_first()
-    wq_follow()
     dkv = wkv_begin()
     dwk_ref[...] = dkv[:, 0:128]
     dwv_ref[...] = dkv[:, 128:256]
+    wq_follow()
     bgt_relays(4, 7)
     wkv_follow()
     gin_ref[...] = (cot_ref[...].astype(F32) + in_second()).astype(BF16)
@@ -654,8 +656,17 @@
 
 
 def settle(*refs):
+    sources, results, held = refs[0:6], refs[6:12], refs[12:18]
+    in_sem, out_sem = refs[18], refs[19]
+    ins = [pltpu.make_async_copy(sources[i], held[i], in_sem.at[i]) for i in range(6)]
+    outs = [pltpu.make_async_copy(held[i], results[i], out_sem.at[i]) for i in range(6)]
+    for copy in ins:
+        copy.start()
     for i in range(6):
-        refs[6 + i][...] = refs[i][...]
+        ins[i].wait()
+        outs[i].start()
+    for copy in outs:
+        copy.wait()
 
 
 def local(inputs, positions, w_query, w_key, w_value, w_out, post_gain, cotangent):
@@ -736,8 +747,9 @@
     hidden, gin, dwq, dwk, dwv, dwo = pl.pallas_call(
         settle,
         out_shape=shapes,
-        in_specs=[vmem] * 6,
-        out_specs=(vmem,) * 6,
+        in_specs=[hbm] * 6,
+        out_specs=(hbm,) * 6,
+        scratch_shapes=[pltpu.VMEM(shape.shape, shape.dtype) for shape in shapes] + [dma((6,)), dma((6,))],
         name="results",
     )(*results)
     return hidden.T, gin.T, dwq, dwk, dwv, dwo.T

time: 158 us -> 158 us (level)
  no operation moved by 1% of the time
where the time goes in v5:
time: 158 us
  Pallas kernels  157 us (99%)
    pallas_call x1, Pallas kernels, local(): pl.pallas_call(kernel, out_shape=shapes, in_specs=[vmem] * 5 + [hbm] * 4,...  155 us

profile of v5, /device:TPU:1, one launch (start us, length us, event | category | flops | bytes accessed | tf_op | source)
XLA Modules:
  0.0 157.7 jit_solution(14931139153014672038)
XLA Ops:
  0.6 154.6 %layer.1 = (bf16[336,256]{1,0:T(8,128)(2,1)}, bf16[336,256]{1,0:T(8,128)(2,1)}, f32[336,256]{1,0:T(8,128)}, f32[336,128]{1,0:T(8,128)}, f32[336,128]{1,0:T(8,128)}, /*index=5*/f32[336,256]{1,0:T(8,128)}) custom-call(bf16[336,256]{1,0:T(8,128)(2,1)} %bitcast.6, bf16[336,256]{1,0:T(8,128)(2,1)} %bitcast.7, s32[1,256]{1,0:T(1,128)} %bitcast.8, ...), custom_call_target="tpu_custom_call" | custom-call | tf_op jit(solution)/shard_map/layer/pallas_call | solution.py:733
  155.3 2.2 %results.1 = (bf16[336,256]{1,0:T(8,128)(2,1)}, bf16[336,256]{1,0:T(8,128)(2,1)}, f32[336,256]{1,0:T(8,128)}, f32[336,128]{1,0:T(8,128)}, f32[336,128]{1,0:T(8,128)}, /*index=5*/f32[336,256]{1,0:T(8,128)}) custom-call(bf16[336,256]{1,0:T(8,128)(2,1)} %get-tuple-element.18.refs_0_, bf16[336,256]{1,0:T(8,128)(2,1)} %get-tuple-element.19.refs_1_, ...), custom_call_target="tpu_custom_call" | custom-call | tf_op jit(solution)/shard_map/results/pallas_call | solution.py:747
